TPU v7x, 32 devices: a whole 2x2x4 slice. The times are simulated.
32 devices in a mesh: fsdp: 32 (over z, y, x, core).
Axes of the slice: x: 2, y: 2, z: 4, core: 2. Of those that a mesh axis runs over, the one named last changes fastest.
Arguments:
- tokens: bfloat16 [8192, 576], P('fsdp'), may hold values from -6 to 6
- segments: int32 [8192], P('fsdp'), may hold values from -1 to 8191, as said below
- w_query: bfloat16 [331776], P('fsdp'), may hold values from -0.25 to 0.25
- w_key: bfloat16 [110592], P('fsdp'), may hold values from -0.25 to 0.25
- w_value: bfloat16 [110592], P('fsdp'), may hold values from -0.25 to 0.25
- w_output: bfloat16 [331776], P('fsdp'), may hold values from -0.75 to 0.75
- w_gate: bfloat16 [884736], P('fsdp'), may hold values from -0.25 to 0.25
- w_up: bfloat16 [884736], P('fsdp'), may hold values from -0.25 to 0.25
- w_down: bfloat16 [884736], P('fsdp'), may hold values from -0.15625 to 0.15625
- gains: bfloat16 [1152], P('fsdp'), may hold values from 0.099609375 to 1.8984375
- cotangent: bfloat16 [8192, 576], P('fsdp'), may hold values from -6 to 6
Outputs:
- output_tokens: bfloat16 [8192, 576], P('fsdp')
- grad_tokens: bfloat16 [8192, 576], P('fsdp')
- grad_query: float32 [331776], P('fsdp')
- grad_key: float32 [110592], P('fsdp')
- grad_value: float32 [110592], P('fsdp')
- grad_output: float32 [331776], P('fsdp')
- grad_gate: float32 [884736], P('fsdp')
- grad_up: float32 [884736], P('fsdp')
- grad_down: float32 [884736], P('fsdp')
- grad_gains: float32 [1152], P('fsdp')
Inputs may be any that keep to these rules, and one draw needn't show every extreme that they name: `segments`: each block of 256 slots holds whole sequences one after another, then -1 in unused slots at its end; a sequence's number is the index in the whole array of its last slot. Every block has at least 64 used slots, the last block is full, and in every draw one block holds a single sequence of 256 tokens.
All inputs are finite; a program needn't handle non-finite values.
Results may differ from a plain program's by a relative error of at most 0.012.
Values may be sent and summed in bfloat16 or wider, within the bound.
A program may use at most 128 MiB of HBM per device.

v0:
```python
import jax
import jax.numpy as jnp
from jax import lax
from jax.sharding import PartitionSpec as P

HEADS = 9
KV_HEADS = 3
HEAD_DIM = 64
FF = 1536
D = 576
KV = 192


ROPE_BASE = 100000.0
NORM_EPSILON = 1e-05
NEG_LARGE = -1e30


def unpack(flat_arrays):
    return (
        flat_arrays[0].reshape(D, D),
        flat_arrays[1].reshape(D, KV),
        flat_arrays[2].reshape(D, KV),
        flat_arrays[3].reshape(D, D),
        flat_arrays[4].reshape(D, FF),
        flat_arrays[5].reshape(D, FF),
        flat_arrays[6].reshape(FF, D),
        flat_arrays[7][:D].astype(jnp.float32),
        flat_arrays[7][D : 2 * D].astype(jnp.float32),
    )


def normalize_parts(values):
    inverse_root = lax.rsqrt(jnp.mean(values * values, axis=-1, keepdims=True) + NORM_EPSILON)
    return (values * inverse_root, inverse_root)


def norm_backward(grad_in, normed, inverse_root, gain_row):
    scaled = grad_in * gain_row
    return inverse_root * (scaled - normed * jnp.mean(scaled * normed, axis=-1, keepdims=True))


def rotate(values, cosine, sine_table):
    half_dim = values.shape[-1] // 2
    first_half = values[..., :half_dim]
    second_half = values[..., half_dim:]
    return jnp.concatenate(
        [
            first_half * cosine - second_half * sine_table,
            second_half * cosine + first_half * sine_table,
        ],
        axis=-1,
    )


def rotate_back(values, cosine, sine_table):
    half_dim = values.shape[-1] // 2
    first_half = values[..., :half_dim]
    second_half = values[..., half_dim:]
    return jnp.concatenate(
        [
            first_half * cosine + second_half * sine_table,
            second_half * cosine - first_half * sine_table,
        ],
        axis=-1,
    )


def per_device(
    tokens, segments, w_query, w_key, w_value, w_output, w_gate, w_up, w_down, gains, cotangent
):
    token_count = tokens.shape[0]
    group_size = HEADS // KV_HEADS
    score_scale = HEAD_DIM ** (-0.5)
    gain_length = gains.shape[0] * lax.axis_size("fsdp")
    gathered = (
        lax.all_gather(w_query, "fsdp", axis=0, tiled=True),
        lax.all_gather(w_key, "fsdp", axis=0, tiled=True),
        lax.all_gather(w_value, "fsdp", axis=0, tiled=True),
        lax.all_gather(w_output, "fsdp", axis=0, tiled=True),
        lax.all_gather(w_gate, "fsdp", axis=0, tiled=True),
        lax.all_gather(w_up, "fsdp", axis=0, tiled=True),
        lax.all_gather(w_down, "fsdp", axis=0, tiled=True),
        lax.all_gather(gains, "fsdp", axis=0, tiled=True),
    )
    (
        query_matrix,
        key_matrix,
        value_matrix,
        output_matrix,
        gate_matrix,
        up_matrix,
        down_matrix,
        gain_first,
        gain_second,
    ) = unpack(gathered)
    column = jnp.arange(token_count)[None, :]
    row_index = jnp.arange(token_count)[:, None]
    same_segment = segments[:, None] == segments[None, :]
    positions = jnp.sum((same_segment & (column < row_index)).astype(jnp.int32), axis=1)
    allowed = same_segment & (column <= row_index)
    frequency = ROPE_BASE ** (-(2.0 * jnp.arange(HEAD_DIM // 2).astype(jnp.float32)) / HEAD_DIM)
    angles = positions.astype(jnp.float32)[:, None] * frequency[None, :]
    cosine = jnp.cos(angles)[:, None, :]
    sine_table = jnp.sin(angles)[:, None, :]
    live_rows = (segments >= 0).astype(jnp.float32)[:, None]
    token_values = tokens.astype(jnp.float32)
    normed_one, root_one = normalize_parts(token_values)
    input_one = (normed_one * gain_first).astype(jnp.bfloat16)
    query_pre = jnp.dot(input_one, query_matrix, preferred_element_type=jnp.float32)
    key_pre = jnp.dot(input_one, key_matrix, preferred_element_type=jnp.float32)
    value_low = jnp.dot(input_one, value_matrix, preferred_element_type=jnp.float32).astype(
        jnp.bfloat16
    )
    value_low = value_low.reshape(token_count, KV_HEADS, HEAD_DIM)
    query_low = rotate(query_pre.reshape(token_count, HEADS, HEAD_DIM), cosine, sine_table).astype(
        jnp.bfloat16
    )
    query_low = query_low.reshape(token_count, KV_HEADS, group_size, HEAD_DIM)
    key_low = rotate(key_pre.reshape(token_count, KV_HEADS, HEAD_DIM), cosine, sine_table).astype(
        jnp.bfloat16
    )
    block_rows = min(token_count, 512)
    block_count = token_count // block_rows

    def masked_scores():
        scores = (
            jnp.einsum("qkgd,tkd->kgqt", query_low, key_low, preferred_element_type=jnp.float32)
            * score_scale
        )
        return (query_low, jnp.where(allowed, scores, NEG_LARGE))

    def attend(block_index):
        query_block, scores = masked_scores()
        row_peak = jnp.max(scores, axis=-1, keepdims=True)
        exponentials = jnp.exp(scores - row_peak)
        totals = jnp.sum(exponentials, axis=-1, keepdims=True)
        probabilities = (exponentials / totals).astype(jnp.bfloat16)
        attended = jnp.einsum(
            "kgqt,tkd->qkgd", probabilities, value_low, preferred_element_type=jnp.float32
        )
        return (attended.astype(jnp.bfloat16), row_peak[..., 0] + jnp.log(totals[..., 0]))

    attended_blocks, log_totals = lax.map(attend, jnp.arange(block_count))
    attended_low = attended_blocks.reshape(token_count, D)
    branch = jnp.dot(attended_low, output_matrix, preferred_element_type=jnp.float32)
    middle = token_values + branch
    normed_two, root_two = normalize_parts(middle)
    input_two = (normed_two * gain_second).astype(jnp.bfloat16)
    gate_pre = jnp.dot(input_two, gate_matrix, preferred_element_type=jnp.float32)
    up_pre = jnp.dot(input_two, up_matrix, preferred_element_type=jnp.float32)
    sigmoid_gate = jax.nn.sigmoid(gate_pre)
    silu_gate = gate_pre * sigmoid_gate
    product_low = (silu_gate * up_pre).astype(jnp.bfloat16)
    result = middle + jnp.dot(product_low, down_matrix, preferred_element_type=jnp.float32)
    output_tokens = (result * live_rows).astype(jnp.bfloat16)
    regathered = (
        lax.all_gather(w_query, "fsdp", axis=0, tiled=True),
        lax.all_gather(w_key, "fsdp", axis=0, tiled=True),
        lax.all_gather(w_value, "fsdp", axis=0, tiled=True),
        lax.all_gather(w_output, "fsdp", axis=0, tiled=True),
        lax.all_gather(w_gate, "fsdp", axis=0, tiled=True),
        lax.all_gather(w_up, "fsdp", axis=0, tiled=True),
        lax.all_gather(w_down, "fsdp", axis=0, tiled=True),
        lax.all_gather(gains, "fsdp", axis=0, tiled=True),
    )
    back_weights = unpack(regathered)
    (
        back_query,
        back_key,
        back_value,
        back_output,
        back_gate,
        back_up,
        back_down,
        back_first,
        back_second,
    ) = back_weights
    grad_result = cotangent.astype(jnp.float32) * live_rows
    grad_down_in = grad_result.astype(jnp.bfloat16)
    grad_down = jnp.einsum(
        "tf,td->fd", product_low, grad_down_in, preferred_element_type=jnp.float32
    )
    grad_product = jnp.einsum(
        "td,fd->tf", grad_down_in, back_down, preferred_element_type=jnp.float32
    )
    grad_gate_pre = (
        grad_product * up_pre * sigmoid_gate * (1.0 + gate_pre * (1.0 - sigmoid_gate))
    ).astype(jnp.bfloat16)
    grad_up_pre = (grad_product * silu_gate).astype(jnp.bfloat16)
    grad_gate = jnp.einsum(
        "td,tf->df", input_two, grad_gate_pre, preferred_element_type=jnp.float32
    )
    grad_up = jnp.einsum("td,tf->df", input_two, grad_up_pre, preferred_element_type=jnp.float32)
    grad_input_two = jnp.einsum(
        "tf,df->td", grad_gate_pre, back_gate, preferred_element_type=jnp.float32
    )
    grad_input_two = grad_input_two + jnp.einsum(
        "tf,df->td", grad_up_pre, back_up, preferred_element_type=jnp.float32
    )
    grad_gain_two = jnp.sum(grad_input_two * normed_two, axis=0)
    grad_middle = grad_result + norm_backward(grad_input_two, normed_two, root_two, back_second)
    grad_branch = grad_middle.astype(jnp.bfloat16)
    grad_output = jnp.einsum(
        "td,te->de", attended_low, grad_branch, preferred_element_type=jnp.float32
    )
    grad_attended = jnp.einsum(
        "te,de->td", grad_branch, back_output, preferred_element_type=jnp.float32
    ).astype(jnp.bfloat16)
    grad_attended = grad_attended.reshape(token_count, KV_HEADS, group_size, HEAD_DIM)

    def back_step(carried, inputs):
        grad_keys, grad_values = carried
        block_index, log_block = inputs
        query_block, scores = masked_scores()
        probabilities = jnp.exp(scores - log_block[..., None])
        grad_probs = jnp.einsum(
            "qkgd,tkd->kgqt", grad_attended, value_low, preferred_element_type=jnp.float32
        )
        centre = jnp.sum(probabilities * grad_probs, axis=-1, keepdims=True)
        grad_scores = (probabilities * (grad_probs - centre)).astype(jnp.bfloat16)
        grad_query_block = (
            jnp.einsum("kgqt,tkd->qkgd", grad_scores, key_low, preferred_element_type=jnp.float32)
            * score_scale
        )
        grad_keys = (
            grad_keys
            + jnp.einsum(
                "kgqt,qkgd->tkd", grad_scores, query_block, preferred_element_type=jnp.float32
            )
            * score_scale
        )
        grad_values = grad_values + jnp.einsum(
            "kgqt,qkgd->tkd",
            probabilities.astype(jnp.bfloat16),
            grad_attended,
            preferred_element_type=jnp.float32,
        )
        return ((grad_keys, grad_values), grad_query_block)

    zero_state = jnp.zeros((token_count, KV_HEADS, HEAD_DIM), jnp.float32)
    (grad_keys, grad_values), grad_query_blocks = lax.scan(
        back_step, (zero_state, zero_state), (jnp.arange(block_count), log_totals)
    )
    grad_query_low = rotate_back(
        grad_query_blocks.reshape(token_count, HEADS, HEAD_DIM), cosine, sine_table
    )
    grad_query_low = grad_query_low.astype(jnp.bfloat16).reshape(token_count, D)
    grad_key_low = (
        rotate_back(grad_keys, cosine, sine_table).astype(jnp.bfloat16).reshape(token_count, KV)
    )
    grad_value_low = grad_values.astype(jnp.bfloat16).reshape(token_count, KV)
    grad_query = jnp.einsum(
        "td,te->de", input_one, grad_query_low, preferred_element_type=jnp.float32
    )
    grad_key = jnp.einsum("td,te->de", input_one, grad_key_low, preferred_element_type=jnp.float32)
    grad_value = jnp.einsum(
        "td,te->de", input_one, grad_value_low, preferred_element_type=jnp.float32
    )
    grad_input_one = jnp.einsum(
        "te,de->td", grad_query_low, back_query, preferred_element_type=jnp.float32
    )
    grad_input_one = grad_input_one + jnp.einsum(
        "te,de->td", grad_key_low, back_key, preferred_element_type=jnp.float32
    )
    grad_input_one = grad_input_one + jnp.einsum(
        "te,de->td", grad_value_low, back_value, preferred_element_type=jnp.float32
    )
    grad_gain_one = jnp.sum(grad_input_one * normed_one, axis=0)
    grad_tokens = grad_middle + norm_backward(grad_input_one, normed_one, root_one, back_first)
    grad_gains = jnp.concatenate(
        [grad_gain_one, grad_gain_two, jnp.zeros((gain_length - 2 * D,), jnp.float32)]
    )
    shares = (
        lax.psum_scatter(grad_query.reshape(-1), "fsdp", scatter_dimension=0, tiled=True),
        lax.psum_scatter(grad_key.reshape(-1), "fsdp", scatter_dimension=0, tiled=True),
        lax.psum_scatter(grad_value.reshape(-1), "fsdp", scatter_dimension=0, tiled=True),
        lax.psum_scatter(grad_output.reshape(-1), "fsdp", scatter_dimension=0, tiled=True),
        lax.psum_scatter(grad_gate.reshape(-1), "fsdp", scatter_dimension=0, tiled=True),
        lax.psum_scatter(grad_up.reshape(-1), "fsdp", scatter_dimension=0, tiled=True),
        lax.psum_scatter(grad_down.reshape(-1), "fsdp", scatter_dimension=0, tiled=True),
        lax.psum_scatter(grad_gains, "fsdp", scatter_dimension=0, tiled=True),
    )
    return (
        output_tokens,
        grad_tokens.astype(jnp.bfloat16),
        shares[0],
        shares[1],
        shares[2],
        shares[3],
        shares[4],
        shares[5],
        shares[6],
        shares[7],
    )


def solution(mesh):
    placed = (
        P("fsdp", None),
        P("fsdp"),
        P("fsdp"),
        P("fsdp"),
        P("fsdp"),
        P("fsdp"),
        P("fsdp"),
        P("fsdp"),
        P("fsdp"),
        P("fsdp"),
        P("fsdp", None),
    )
    return jax.shard_map(
        per_device,
        mesh=mesh,
        in_specs=placed,
        out_specs=(
            P("fsdp", None),
            P("fsdp", None),
            P("fsdp"),
            P("fsdp"),
            P("fsdp"),
            P("fsdp"),
            P("fsdp"),
            P("fsdp"),
            P("fsdp"),
            P("fsdp"),
        ),
        check_vma=False,
    )
```

profile of v0, /device:TPU:0, one launch (start us, length us, event | category | flops | bytes accessed | tf_op | source)
XLA Modules:
  0.0 576.0 jit_solution(10126677412886435707)
XLA Ops:
  7.2 0.7 all-gather.8.cloned.1.call-update
  8.0 0.7 all-gather.10.cloned.1.call-update
  8.7 0.7 all-gather.12.cloned.1.call-update
  9.5 0.9 convert_reduce_fusion
  10.3 1.1 fusion.30
  11.4 0.9 dynamic-update-slice
  12.3 42.1 %all-reduce = bf16[1152]{0:T(1024)(128)(2,1)S(1)} all-reduce(bf16[1152]{0:T(1024)(128)(2,1)S(1)} %dynamic-update-slice), channel_id=1, replica_groups=mesh['fsdp'=32] {'fsdp'}, use_global_device_ids=true, to_apply=%add | all-reduce | flops 1152 | bytes 4608
  54.4 0.7 slice_convert_fusion
  55.0 0.7 reshape.232
  55.7 0.7 reshape.230
  56.4 0.8 reshape.234
  57.2 0.8 reshape.236
  58.0 41.8 %all-gather = bf16[32,1,3456]{2,1,0:T(2,128)(2,1)S(1)} all-gather(bf16[1,1,3456]{2,1,0:T(2,128)(2,1)S(1)} %reshape.230), channel_id=1, replica_groups=mesh['fsdp'=32] {'fsdp'}, dimensions={0}, use_global_device_ids=true | all-gather | bytes 228096 | tf_op jit(solution)/shard_map/all_gather | solution.py:79
  99.8 1.3 reduce
  101.3 38.2 %all-gather.1 = bf16[32,1,3456]{2,1,0:T(2,128)(2,1)S(1)} all-gather(bf16[1,1,3456]{2,1,0:T(2,128)(2,1)S(1)} %reshape.232), channel_id=1, replica_groups=mesh['fsdp'=32] {'fsdp'}, dimensions={0}, use_global_device_ids=true | all-gather | bytes 228096 | tf_op jit(solution)/shard_map/all_gather | solution.py:78
  139.5 1.3 reduce.1
  141.2 43.8 %all-gather.3 = bf16[32,1,10368]{2,1,0:T(2,128)(2,1)S(1)} all-gather(bf16[1,1,10368]{2,1,0:T(2,128)(2,1)S(1)} %reshape.236), channel_id=1, replica_groups=mesh['fsdp'=32] {'fsdp'}, dimensions={0}, use_global_device_ids=true | all-gather | bytes 684288 | tf_op jit(solution)/shard_map/all_gather | solution.py:80
  185.0 4.0 reduce.3
  189.0 1.7 reshape.214
  190.8 40.5 %all-gather.2 = bf16[32,1,10368]{2,1,0:T(2,128)(2,1)S(1)} all-gather(bf16[1,1,10368]{2,1,0:T(2,128)(2,1)S(1)} %reshape.234), channel_id=1, replica_groups=mesh['fsdp'=32] {'fsdp'}, dimensions={0}, use_global_device_ids=true | all-gather | bytes 684288 | tf_op jit(solution)/shard_map/all_gather | solution.py:77
  231.3 4.0 reduce.2
  235.3 0.9 reshape.212
  238.6 0.5 fusion.55
  239.5 0.6 compare_convert_fusion
  240.5 0.5 convolution_convert_fusion
  241.1 0.5 copy-done.7
  242.8 4.6 reshape.215
  247.5 4.5 reshape.216
  251.9 3.6 fusion.57
  255.5 2.0 fusion.56
  257.5 4.3 reshape.217
  261.8 4.8 multiply_convert_fusion
  266.6 0.7 fusion.58
  267.3 0.8 copy-done.3
  268.1 1.4 multiply_reduce_fusion
  269.7 0.9 copy-done.8
  271.0 1.6 fusion.40
  272.6 0.5 fusion.16
  273.5 0.6 fusion
  275.1 1.2 fusion.15
  276.6 2.5 fusion.60
  279.1 2.4 fusion.59
  281.8 1.1 reshape.223
  282.9 1.7 reshape.224
  285.0 1.1 reshape.222
  286.6 1.7 reshape.221
  288.3 4.9 reshape.226
  293.2 4.7 reshape.225
  297.9 2.8 fusion.36
  300.6 5.3 reshape.227
  306.0 0.9 copy-done.15
  307.6 2.2 fusion.29
  309.9 38.8 %all-reduce.8 = f32[1152]{0:T(1024)S(1)} all-reduce(f32[1152]{0:T(1024)S(1)} %pad_maximum_fusion.3), channel_id=9, replica_groups=mesh['fsdp'=32] {'fsdp'}, use_global_device_ids=true, to_apply=%region_17.18.clone | all-reduce | flops 1152 | bytes 9216
  348.7 0.6 dynamic-slice.8
  349.3 1.9 fusion.28
  351.2 1.6 fusion.7
  352.8 205.7 %all-reduce.12.cloned.1.call-done = (f32[331776]{0:T(1024)}, f32[110592]{0:T(1024)}, f32[110592]{0:T(1024)}, f32[331776]{0:T(1024)}, f32[884736]{0:T(1024)}, /*index=5*/f32[884736]{0:T(1024)}, f32[884736]{0:T(1024)}) async-done(((f32[331776]{0:T(1024)}, f32[110592]{0:T(1024)}, f32[110592]{0:T(1024)}, f32[331776]{0:T(1024)}, f32[884736]{0:T(1024)}, /*index=5*/f32[884736]{0:T(1024)}, f32[884736]{0:T(1024)}), ...) | async-done | bytes 14155792
  558.6 1.5 dynamic-slice.1
  560.1 1.5 dynamic-slice.4
  561.6 1.4 dynamic-slice.2
  563.0 1.4 dynamic-slice.3
  564.4 1.5 dynamic-slice.5
  565.9 1.5 dynamic-slice.6
  567.5 1.5 dynamic-slice.7
  (136 shorter events, 9.3 us)
Async XLA Ops:
  7.2 235.6 %all-gather.8.cloned.1.call-start = ((), (), s32[]{:S(2)}) async-start(), calls=%async_computation | async-start | bytes 1824768 | tf_op jit(solution)/shard_map/all_gather | solution.py:81
  7.9 239.6 %all-gather.10.cloned.1.call-start = ((), (), s32[]{:S(2)}) async-start(), calls=%async_computation.1 | async-start | bytes 1824768 | tf_op jit(solution)/shard_map/all_gather | solution.py:82
  8.7 248.8 %all-gather.12.cloned.1.call-start = ((), (), s32[]{:S(2)}) async-start(), calls=%async_computation.2 | async-start | bytes 1824768 | tf_op jit(solution)/shard_map/all_gather | solution.py:83
  9.4 549.2 %all-reduce.12.cloned.1.call-start = ((), (), s32[]{:S(2)}) async-start(), calls=%async_computation.3 | async-start | bytes 28311552
  11.4 228.6 %copy-start.40 = (f32[256]{0:T(256)}, f32[256]{0:T(256)S(1)}, u32[]{:S(2)}) copy-start(f32[256]{0:T(256)S(1)} %add_rsqrt_fusion.1) | copy-start | bytes 3076
  101.3 138.8 %copy-start.18 = (bf16[576,192]{1,0:T(8,128)(2,1)}, bf16[576,192]{1,0:T(8,128)(2,1)S(1)}, u32[]{:S(2)}) copy-start(bf16[576,192]{1,0:T(8,128)(2,1)S(1)} %reshape.209) | copy-start | bytes 663556
  141.0 48.0 %copy-start.14 = (bf16[576,192]{1,0:T(8,128)(2,1)}, bf16[576,192]{1,0:T(8,128)(2,1)S(1)}, u32[]{:S(2)}) copy-start(bf16[576,192]{1,0:T(8,128)(2,1)S(1)} %reshape.211) | copy-start | bytes 663556
  235.3 1.3 copy-start
  236.2 1.2 copy-start.9
  236.5 1.2 copy-start.44
  237.6 0.6 copy-start.23
  237.6 0.6 copy-start.25
  237.7 1.4 copy-start.32
  237.7 1.4 copy-start.34
  237.9 0.7 copy-start.28
  237.9 1.2 copy-start.30
  240.5 0.6 copy-start.38
  240.5 1.2 copy-start.7
  241.1 1.0 copy-start.16
  241.1 1.5 copy-start.36
  242.1 0.5 copy-start.42
  251.9 3.6 copy-start.1
  261.8 4.9 copy-start.2
  266.6 1.5 copy-start.3
  266.6 1.5 copy-start.37
  266.6 1.5 copy-start.43
  268.1 1.4 copy-start.19
  268.1 1.4 copy-start.46
  269.5 1.1 copy-start.8
  269.5 1.5 copy-start.17
  270.6 2.0 copy-start.4
  272.6 0.9 copy-start.39
  273.5 8.0 %copy-start.21 = (bf16[3,64,256]{2,1,0:T(8,128)(2,1)}, bf16[3,64,256]{2,1,0:T(8,128)(2,1)S(1)}, u32[]{:S(2)}) copy-start(bf16[3,64,256]{2,1,0:T(8,128)(2,1)S(1)} %fusion.16) | copy-start | bytes 294916
  274.1 0.9 copy-start.29
  274.1 1.0 copy-start.31
  274.1 2.2 copy-start.33
  274.1 2.1 copy-start.35
  279.1 2.4 copy-start.41
  281.5 1.4 copy-start.11
  282.9 1.7 copy-start.24
  282.9 1.7 copy-start.26
  282.9 1.7 copy-start.27
  293.2 4.7 copy-start.12
  293.2 4.7 copy-start.20
  293.2 4.7 copy-start.47
  305.9 1.0 copy-start.15
  305.9 1.2 copy-start.10
  306.0 1.6 copy-start.22
  307.2 2.7 copy-start.45
  307.2 42.1 %copy-start.5 = (f32[256,576]{0,1:T(8,128)S(1)}, f32[256,576]{0,1:T(8,128)}, u32[]{:S(2)}) copy-start(f32[256,576]{0,1:T(8,128)} %copy-done.4) | copy-start | bytes 1769476
  307.6 43.6 %copy-start.6 = (bf16[1536,576]{1,0:T(8,128)(2,1)S(1)}, bf16[1536,576]{1,0:T(8,128)(2,1)}, u32[]{:S(2)}) copy-start(bf16[1536,576]{1,0:T(8,128)(2,1)} %reshape.217) | copy-start | bytes 5308420
  348.7 2.5 copy-start.13
Sparse Core Ops, SparseCore 0:
  10.8 58.4 all-gather.7
  72.1 54.7 all-gather.9
  129.8 56.8 all-gather.11
  306.1 252.4 all-reduce.11
where the time goes:
time: 585 us; the launch traced here: 576 us
  blocking collectives  245 us (42%)
  waiting for transfers between devices  208 us (36%)
  local copies, waits for them, and re-layouts  57.7 us (10%)
  matrix products  32.9 us (6%)
  other arithmetic  17.4 us (3%)
  between operations  14.8 us (3%)
    unnamed x5, waiting for transfers between devices  208 us
    unnamed x2, blocking collectives  80.8 us
    all_gather x1, blocking collectives, per_device(): lax.all_gather(w_output, 'fsdp', axis=0, tiled=True)  43.8 us
    all_gather x1, blocking collectives, per_device(): lax.all_gather(w_value, 'fsdp', axis=0, tiled=True)  41.8 us
    all_gather x1, blocking collectives, per_device(): lax.all_gather(w_query, 'fsdp', axis=0, tiled=True)  40.5 us
    all_gather x1, blocking collectives, per_device(): lax.all_gather(w_key, 'fsdp', axis=0, tiled=True)  38.2 us
    unnamed x110, local copies, waits for them, and re-layouts  20.2 us
  transfers between devices with their start and end apart: 4, of which 1 were waited for; matrix products, arithmetic and copies ran while one was open for 8% of the time, Pallas kernels for 0%

commit v1 on v0

--- a/solution.py
+++ b/solution.py
@@ -1,6 +1,10 @@
 import jax
 import jax.numpy as jnp
+import ml_dtypes
+import numpy as np
 from jax import lax
+from jax.experimental import pallas as pl
+from jax.experimental.pallas import tpu as pltpu
 from jax.sharding import PartitionSpec as P
 
 HEADS = 9
@@ -295,6 +299,442 @@
     )
 
 
+AXIS_SIZES = (4, 2, 2, 2)
+ORDERS = ((1, 0, 2), (0, 2, 1), (2, 0, 1), (0, 1, 2))
+ARRAYS = 4
+WIDE = 1536
+NARROW = 640
+SHAPES = ((16, WIDE), (16, WIDE), (16, WIDE), (64, NARROW))
+MESH = pl.DeviceIdType.MESH
+
+
+def coordinates():
+    me = lax.axis_index("fsdp")
+    return [me // 8, (me // 4) % 2, (me // 2) % 2, me % 2]
+
+
+def device_at(coords):
+    return ((coords[0] * 2 + coords[1]) * 2 + coords[2]) * 2 + coords[3]
+
+
+def peers_along(coords, dim):
+    found = []
+    for offset in range(1, AXIS_SIZES[dim]):
+        other = list(coords)
+        other[dim] = lax.rem(coords[dim] + offset, AXIS_SIZES[dim])
+        found.append(other)
+    return found
+
+
+def enter(coords):
+    barrier = pltpu.get_barrier_semaphore()
+    count = 0
+    for dim in range(4):
+        for other in peers_along(coords, dim):
+            pl.semaphore_signal(barrier, inc=1, device_id=(device_at(other),), device_id_type=MESH)
+            count += 1
+    pl.semaphore_wait(barrier, count)
+
+
+def gather_kernel(*refs):
+    ins, outs = refs[:ARRAYS], refs[ARRAYS : 2 * ARRAYS]
+    send_sem, recv_sem = refs[2 * ARRAYS :]
+    coords = coordinates()
+    enter(coords)
+
+    def run(which):
+        out = outs[which]
+        out[coords[0], coords[1], coords[2], coords[3]] = ins[which][...]
+        counter = [0]
+        index = list(coords)
+        sibling = peers_along(coords, 3)[0]
+        core_copies = []
+
+        def push(block, target):
+            slot = counter[0]
+            counter[0] += 1
+            view = out.at[tuple(block)]
+            copy = pltpu.make_async_remote_copy(
+                src_ref=view,
+                dst_ref=view,
+                send_sem=send_sem.at[which, slot],
+                recv_sem=recv_sem.at[which, slot],
+                device_id=(device_at(target),),
+                device_id_type=MESH,
+            )
+            copy.start()
+            return copy
+
+        pending_core = [list(index)]
+        for dim in ORDERS[which]:
+            copies = [push(index, other) for other in peers_along(coords, dim)]
+            for block in pending_core:
+                core_copies.append(push(block, sibling))
+            pending_core = []
+            yield
+            for offset, copy in enumerate(copies):
+                copy.wait()
+                block = list(index)
+                size = AXIS_SIZES[dim]
+                block[dim] = lax.rem(coords[dim] + size - offset - 1, size)
+                pending_core.append(block)
+            index[dim] = slice(None)
+        for block in pending_core:
+            core_copies.append(push(block, sibling))
+        yield
+        for copy in core_copies:
+            copy.wait()
+
+    drive([run(which) for which in range(ARRAYS)])
+
+
+def drive(tasks):
+    while tasks:
+        kept = []
+        for task in tasks:
+            try:
+                next(task)
+                kept.append(task)
+            except StopIteration:
+                pass
+        tasks = kept
+
+
+def scatter_kernel(*refs):
+    ins, outs = refs[:ARRAYS], refs[ARRAYS : 2 * ARRAYS]
+    landing = refs[2 * ARRAYS : 6 * ARRAYS]
+    send_sem, recv_sem = refs[6 * ARRAYS :]
+    coords = coordinates()
+    enter(coords)
+
+    def run(which):
+        order = (3,) + tuple(reversed(ORDERS[which]))
+        remaining = [0, 1, 2, 3]
+        current = ins[which]
+        counter = [0]
+
+        def push(stage, dim, part, offset, target):
+            slot = counter[0]
+            counter[0] += 1
+            index = tuple(
+                part if axis == dim else slice(None) for axis in remaining
+            )
+            land = landing[which * 4 + stage]
+            copy = pltpu.make_async_remote_copy(
+                src_ref=current.at[index],
+                dst_ref=land.at[offset],
+                send_sem=send_sem.at[which, slot],
+                recv_sem=recv_sem.at[which, slot],
+                device_id=(device_at(target),),
+                device_id_type=MESH,
+            )
+            copy.start()
+            return copy
+
+        copies = [
+            push(0, 3, other[3], offset, other)
+            for offset, other in enumerate(peers_along(coords, 3))
+        ]
+        for stage, dim in enumerate(order):
+            yield
+            for copy in copies:
+                copy.wait()
+            land = landing[which * 4 + stage]
+            rest = [axis for axis in remaining if axis != dim]
+            last = stage == 3
+
+            def add_group(fixed, current=current, land=land, rest=rest, dim=dim, last=last, held=tuple(remaining)):
+                loose = [axis for axis in rest if axis not in fixed]
+                total = 1
+                for axis in loose:
+                    total *= AXIS_SIZES[axis]
+
+                def body(step, carry):
+                    at = dict(fixed)
+                    left = step
+                    for axis in reversed(loose):
+                        at[axis] = left % AXIS_SIZES[axis]
+                        left = left // AXIS_SIZES[axis]
+                    mine = tuple(coords[dim] if axis == dim else at[axis] for axis in held)
+                    target = tuple(at[axis] for axis in rest)
+                    value = current[mine].astype(jnp.float32)
+                    for offset in range(AXIS_SIZES[dim] - 1):
+                        value = value + land[(offset,) + target].astype(jnp.float32)
+                    if last:
+                        outs[which][...] = value
+                    else:
+                        land[(0,) + target] = value.astype(jnp.bfloat16)
+                    return carry
+
+                if total == 1:
+                    body(0, 0)
+                else:
+                    lax.fori_loop(0, total, body, 0)
+
+            if last:
+                add_group({})
+                break
+            following = order[stage + 1]
+            remaining = rest
+            current = land.at[0]
+            copies = []
+            for offset, other in enumerate(peers_along(coords, following)):
+                add_group({following: other[following]})
+                copies.append(push(stage + 1, following, other[following], offset, other))
+            add_group({following: coords[following]})
+
+    drive([run(which) for which in range(ARRAYS)])
+
+
+def gather_packed(parts):
+    return pl.pallas_call(
+        gather_kernel,
+        out_shape=tuple(jax.ShapeDtypeStruct(AXIS_SIZES + shape, jnp.bfloat16) for shape in SHAPES),
+        in_specs=[pl.BlockSpec(memory_space=pltpu.VMEM)] * ARRAYS,
+        out_specs=tuple([pl.BlockSpec(memory_space=pltpu.VMEM)] * ARRAYS),
+        scratch_shapes=[
+            pltpu.SemaphoreType.DMA((ARRAYS, 12)),
+            pltpu.SemaphoreType.DMA((ARRAYS, 12)),
+        ],
+        compiler_params=pltpu.CompilerParams(
+            collective_id=0, has_side_effects=True, vmem_limit_bytes=32 * 1024 * 1024
+        ),
+        name="gather_weights",
+    )(*parts)
+
+
+def scatter_packed(parts):
+    landing = []
+    for which in range(ARRAYS):
+        remaining = [0, 1, 2, 3]
+        for dim in (3,) + tuple(reversed(ORDERS[which])):
+            remaining = [axis for axis in remaining if axis != dim]
+            extent = tuple(AXIS_SIZES[axis] for axis in remaining)
+            landing.append(
+                pltpu.VMEM((AXIS_SIZES[dim] - 1,) + extent + SHAPES[which], jnp.bfloat16)
+            )
+    return pl.pallas_call(
+        scatter_kernel,
+        out_shape=tuple(jax.ShapeDtypeStruct(shape, jnp.float32) for shape in SHAPES),
+        in_specs=[pl.BlockSpec(memory_space=pltpu.VMEM)] * ARRAYS,
+        out_specs=tuple([pl.BlockSpec(memory_space=pltpu.VMEM)] * ARRAYS),
+        scratch_shapes=landing
+        + [
+            pltpu.SemaphoreType.DMA((ARRAYS, 8)),
+            pltpu.SemaphoreType.DMA((ARRAYS, 8)),
+        ],
+        compiler_params=pltpu.CompilerParams(
+            collective_id=1, has_side_effects=True, vmem_limit_bytes=40 * 1024 * 1024
+        ),
+        name="scatter_gradients",
+    )(*parts)
+
+
+DEVICES = 32
+ROWS = D // DEVICES
+DOWN_ROWS = FF // DEVICES
+SPILL = ROWS - 16
+
+
+def order_matrix():
+    true_index = np.concatenate(
+        [
+            (np.arange(DEVICES)[:, None] * ROWS + np.arange(16)[None, :]).reshape(-1),
+            (np.arange(DEVICES)[:, None] * ROWS + 16 + np.arange(SPILL)[None, :]).reshape(-1),
+        ]
+    )
+    matrix = np.zeros((D, D), np.float32)
+    matrix[true_index, np.arange(D)] = 1.0
+    return matrix.astype(ml_dtypes.bfloat16)
+
+
+def dot(left, right, contract=(1, 0), precision=None):
+    return lax.dot_general(
+        left,
+        right,
+        (((contract[0],), (contract[1],)), ((), ())),
+        preferred_element_type=jnp.float32,
+        precision=precision,
+    )
+
+
+def low_dot(left, right, contract=(1, 0)):
+    return dot(left, right, contract).astype(jnp.bfloat16)
+
+
+def packed_device(
+    tokens, segments, w_query, w_key, w_value, w_output, w_gate, w_up, w_down, gains, cotangent
+):
+    token_count = tokens.shape[0]
+    group_size = HEADS // KV_HEADS
+    score_scale = HEAD_DIM ** (-0.5)
+    order = jnp.asarray(order_matrix())
+    rows = jnp.concatenate(
+        [
+            w_query.reshape(ROWS, D),
+            w_key.reshape(ROWS, KV),
+            w_value.reshape(ROWS, KV),
+            low_dot(w_output.reshape(ROWS, D), order),
+            w_gate.reshape(ROWS, FF),
+            w_up.reshape(ROWS, FF),
+        ],
+        axis=1,
+    )
+    down_rows = low_dot(w_down.reshape(DOWN_ROWS, D), order)
+    share = gains.shape[0]
+    spare = jnp.pad(gains.reshape(1, share), ((0, 63), (0, 64 - share)))
+    extra = jnp.concatenate(
+        [jnp.concatenate([rows[16:].reshape(16, D), down_rows], axis=0), spare], axis=1
+    )
+    mixed, gate_part, up_part, extra_all = gather_packed(
+        (rows[:16, :WIDE], rows[:16, WIDE : 2 * WIDE], rows[:16, 2 * WIDE :], extra)
+    )
+    extra_all = extra_all.reshape(DEVICES, 64, NARROW)
+    spill = extra_all[:, :16, :D].reshape(DEVICES * SPILL, 3 * WIDE)
+    mixed = jnp.concatenate([mixed.reshape(512, WIDE), spill[:, :WIDE]], axis=0)
+    gate_matrix = jnp.concatenate([gate_part.reshape(512, WIDE), spill[:, WIDE : 2 * WIDE]], axis=0)
+    up_matrix = jnp.concatenate([up_part.reshape(512, WIDE), spill[:, 2 * WIDE :]], axis=0)
+    down_matrix = extra_all[:, 16:, :D].reshape(FF, D)
+    gain_all = extra_all[:, 0, D : D + share].reshape(2, D)
+    gain_rows = dot(gain_all, order)
+    gain_first, gain_second = gain_rows[0:1], gain_rows[1:2]
+    qkv_matrix = mixed[:, : D + 2 * KV]
+    output_matrix = mixed[:, D + 2 * KV :]
+
+    column = jnp.arange(token_count)[None, :]
+    row_index = jnp.arange(token_count)[:, None]
+    same_segment = segments[:, None] == segments[None, :]
+    positions = jnp.sum((same_segment & (column < row_index)).astype(jnp.int32), axis=1)
+    allowed = same_segment & (column <= row_index)
+    frequency = ROPE_BASE ** (-(2.0 * jnp.arange(HEAD_DIM // 2).astype(jnp.float32)) / HEAD_DIM)
+    angles = positions.astype(jnp.float32)[:, None] * frequency[None, :]
+    cosine = jnp.cos(angles)[:, None, :]
+    sine_table = jnp.sin(angles)[:, None, :]
+    live_rows = (segments >= 0).astype(jnp.float32)[:, None]
+
+    token_values = dot(tokens, order)
+    grad_result = dot(cotangent, order) * live_rows
+    grad_down_in = grad_result.astype(jnp.bfloat16)
+
+    normed_one, root_one = normalize_parts(token_values)
+    input_one = (normed_one * gain_first).astype(jnp.bfloat16)
+    qkv = dot(input_one, qkv_matrix)
+    query_pre, key_pre = qkv[:, :D], qkv[:, D : D + KV]
+    value_low = qkv[:, D + KV :].astype(jnp.bfloat16).reshape(token_count, KV_HEADS, HEAD_DIM)
+    query_low = rotate(query_pre.reshape(token_count, HEADS, HEAD_DIM), cosine, sine_table).astype(
+        jnp.bfloat16
+    )
+    query_low = query_low.reshape(token_count, KV_HEADS, group_size, HEAD_DIM)
+    key_low = rotate(key_pre.reshape(token_count, KV_HEADS, HEAD_DIM), cosine, sine_table).astype(
+        jnp.bfloat16
+    )
+    scores = (
+        jnp.einsum("qkgd,tkd->kgqt", query_low, key_low, preferred_element_type=jnp.float32)
+        * score_scale
+    )
+    scores = jnp.where(allowed, scores, NEG_LARGE)
+    row_peak = jnp.max(scores, axis=-1, keepdims=True)
+    exponentials = jnp.exp(scores - row_peak)
+    totals = jnp.sum(exponentials, axis=-1, keepdims=True)
+    probabilities = exponentials / totals
+    probs_low = probabilities.astype(jnp.bfloat16)
+    attended = jnp.einsum("kgqt,tkd->qkgd", probs_low, value_low, preferred_element_type=jnp.float32)
+    attended_low = low_dot(attended.astype(jnp.bfloat16).reshape(token_count, D), order)
+    middle = token_values + dot(attended_low, output_matrix)
+    normed_two, root_two = normalize_parts(middle)
+    input_two = (normed_two * gain_second).astype(jnp.bfloat16)
+    gate_pre = dot(input_two, gate_matrix)
+    up_pre = dot(input_two, up_matrix)
+    sigmoid_gate = jax.nn.sigmoid(gate_pre)
+    silu_gate = gate_pre * sigmoid_gate
+    product_low = (silu_gate * up_pre).astype(jnp.bfloat16)
+    result = middle + dot(product_low, down_matrix)
+    output_tokens = low_dot((result * live_rows).astype(jnp.bfloat16), order, (1, 1))
+
+    grad_down = low_dot(product_low, grad_down_in, (0, 0))
+    grad_product = dot(grad_down_in, down_matrix, (1, 1))
+    grad_gate_pre = (
+        grad_product * up_pre * sigmoid_gate * (1.0 + gate_pre * (1.0 - sigmoid_gate))
+    ).astype(jnp.bfloat16)
+    grad_up_pre = (grad_product * silu_gate).astype(jnp.bfloat16)
+    grad_gate = low_dot(input_two, grad_gate_pre, (0, 0))
+    grad_up = low_dot(input_two, grad_up_pre, (0, 0))
+    grad_input_two = dot(grad_gate_pre, gate_matrix, (1, 1)) + dot(grad_up_pre, up_matrix, (1, 1))
+    grad_gain_two = jnp.sum(grad_input_two * normed_two, axis=0)
+    grad_middle = grad_result + norm_backward(grad_input_two, normed_two, root_two, gain_second)
+    grad_branch = grad_middle.astype(jnp.bfloat16)
+    grad_output = low_dot(attended_low, grad_branch, (0, 0))
+    grad_attended = low_dot(low_dot(grad_branch, output_matrix, (1, 1)), order, (1, 1))
+    grad_attended = grad_attended.reshape(token_count, KV_HEADS, group_size, HEAD_DIM)
+
+    grad_probs = jnp.einsum(
+        "qkgd,tkd->kgqt", grad_attended, value_low, preferred_element_type=jnp.float32
+    )
+    centre = jnp.sum(probabilities * grad_probs, axis=-1, keepdims=True)
+    grad_scores = (probabilities * (grad_probs - centre)).astype(jnp.bfloat16)
+    grad_queries = (
+        jnp.einsum("kgqt,tkd->qkgd", grad_scores, key_low, preferred_element_type=jnp.float32)
+        * score_scale
+    )
+    grad_keys = (
+        jnp.einsum("kgqt,qkgd->tkd", grad_scores, query_low, preferred_element_type=jnp.float32)
+        * score_scale
+    )
+    grad_values = jnp.einsum(
+        "kgqt,qkgd->tkd", probs_low, grad_attended, preferred_element_type=jnp.float32
+    )
+    grad_query_low = rotate_back(
+        grad_queries.reshape(token_count, HEADS, HEAD_DIM), cosine, sine_table
+    )
+    grad_qkv = jnp.concatenate(
+        [
+            grad_query_low.astype(jnp.bfloat16).reshape(token_count, D),
+            rotate_back(grad_keys, cosine, sine_table).astype(jnp.bfloat16).reshape(token_count, KV),
+            grad_values.astype(jnp.bfloat16).reshape(token_count, KV),
+        ],
+        axis=1,
+    )
+    grad_mixed = jnp.concatenate([low_dot(input_one, grad_qkv, (0, 0)), grad_output], axis=1)
+    grad_input_one = dot(grad_qkv, qkv_matrix, (1, 1))
+    grad_gain_one = jnp.sum(grad_input_one * normed_one, axis=0)
+    grad_tokens = grad_middle + norm_backward(grad_input_one, normed_one, root_one, gain_first)
+    grad_tokens = low_dot(grad_tokens.astype(jnp.bfloat16), order, (1, 1))
+
+    grad_gains = low_dot(jnp.stack([grad_gain_one, grad_gain_two]).astype(jnp.bfloat16), order, (1, 1))
+    grad_gains = jnp.pad(
+        grad_gains.reshape(DEVICES, 1, share), ((0, 0), (0, 63), (0, 64 - share))
+    )
+    spill = jnp.concatenate([grad_mixed[512:], grad_gate[512:], grad_up[512:]], axis=1)
+    extra = jnp.concatenate(
+        [spill.reshape(DEVICES, 16, D), grad_down.reshape(DEVICES, DOWN_ROWS, D)], axis=1
+    )
+    extra = jnp.concatenate([extra, grad_gains], axis=2)
+    mixed, gate_part, up_part, extra = scatter_packed(
+        (
+            grad_mixed[:512].reshape(AXIS_SIZES + SHAPES[0]),
+            grad_gate[:512].reshape(AXIS_SIZES + SHAPES[1]),
+            grad_up[:512].reshape(AXIS_SIZES + SHAPES[2]),
+            extra.reshape(AXIS_SIZES + SHAPES[3]),
+        )
+    )
+    spill = extra[:16, :D].reshape(SPILL, 3 * WIDE)
+    mixed = jnp.concatenate([mixed, spill[:, :WIDE]], axis=0)
+    exact = lax.Precision.HIGHEST
+    wide_order = order.astype(jnp.float32)
+    return (
+        output_tokens,
+        grad_tokens,
+        mixed[:, :D].reshape(-1),
+        mixed[:, D : D + KV].reshape(-1),
+        mixed[:, D + KV : D + 2 * KV].reshape(-1),
+        dot(mixed[:, D + 2 * KV :], wide_order, (1, 1), exact).reshape(-1),
+        jnp.concatenate([gate_part, spill[:, WIDE : 2 * WIDE]], axis=0).reshape(-1),
+        jnp.concatenate([up_part, spill[:, 2 * WIDE :]], axis=0).reshape(-1),
+        dot(extra[16:, :D], wide_order, (1, 1), exact).reshape(-1),
+        extra[0, D : D + share],
+    )
+
+
 def solution(mesh):
     placed = (
         P("fsdp", None),
@@ -310,7 +750,7 @@
         P("fsdp", None),
     )
     return jax.shard_map(
-        per_device,
+        packed_device if mesh.shape["fsdp"] == DEVICES else per_device,
         mesh=mesh,
         in_specs=placed,
         out_specs=(

time: 585 us -> 207 us (0.35); the launches traced: 576 us -> 206 us
  blocking collectives: 245 us -> 0 us
  waiting for transfers between devices: 208 us -> 0 us
  Pallas kernels: 0 us -> 102 us
  matrix products: 32.9 us -> 48.1 us
  local copies, waits for them, and re-layouts: 57.7 us -> 43.9 us
  between operations: 14.8 us -> 1.5 us
  other arithmetic: 17.4 us -> 10.2 us
    unnamed x5 -> x0, waiting for transfers between devices: 208 us -> none
    all_gather x4 -> x0, blocking collectives: 164 us -> none  [the longest x1 43.8 us: per_device(): lax.all_gather(w_output, 'fsdp', axis=0, tiled=True)]
    pallas_call x0 -> x2, Pallas kernels: none -> 102 us  [the longest x1 53.7 us: gather_packed(): pl.pallas_call(gather_kernel, out_shape=tuple((jax.ShapeDtypeStruct(AXIS_...]
    unnamed x2 -> x0, blocking collectives: 80.8 us -> none
    reshape x14 -> x19, local copies, waits for them, and re-layouts: 36.9 us -> 13.4 us  [the longest x1 2.25 us: packed_device(): spill = extra_all[:, :16, :D].reshape(DEVICES * SPILL, 3 * WIDE)]
    slice x0 -> x22, local copies, waits for them, and re-layouts: none -> 12.2 us  [the longest x1 3.04 us: packed_device(): down_matrix = extra_all[:, 16:, :D].reshape(FF, D)]
    dot_general x27 -> x30, matrix products: 32.9 us -> 44.2 us  [the longest x25 37 us: dot(): lax.dot_general(left, right, (((contract[0],), (contract[1],)), ((), ()))...]
    all_gather x4 -> x0, other arithmetic: 10.5 us -> none  [the longest x1 3.96 us: per_device(): lax.all_gather(w_query, 'fsdp', axis=0, tiled=True)]
  transfers between devices with their start and end apart: 4 -> 0, of which waited for: 1 -> 0; matrix products, arithmetic and copies ran while one was open for 8% -> 0% of each run, Pallas kernels for 0% -> 0%
where the time goes in v1:
time: 207 us; the launch traced here: 206 us
  Pallas kernels  102 us (49%)
  matrix products  48.1 us (23%)
  local copies, waits for them, and re-layouts  43.9 us (21%)
  other arithmetic  10.2 us (5%)
    pallas_call x1, Pallas kernels, gather_packed(): pl.pallas_call(gather_kernel, out_shape=tuple((jax.ShapeDtypeStruct(AXIS_...  53.7 us
    pallas_call x1, Pallas kernels, scatter_packed(): pl.pallas_call(scatter_kernel, out_shape=tuple((jax.ShapeDtypeStruct(shap...  48.3 us
    dot_general x25, matrix products, dot(): lax.dot_general(left, right, (((contract[0],), (contract[1],)), ((), ()))...  37 us
    unnamed x148, local copies, waits for them, and re-layouts  12.9 us

profile of v1, /device:TPU:0, one launch (start us, length us, event | category | flops | bytes accessed | tf_op | source)
XLA Modules:
  0.0 205.7 jit_solution(12678768264381401419)
XLA Ops:
  0.7 0.7 compare_convert_fusion
  1.4 0.9 convert_reduce_fusion
  2.3 0.8 reshape.249
  3.1 0.8 reshape.250
  3.9 0.8 reshape.248
  4.7 0.8 reshape.251
  5.6 1.4 fusion.23
  7.0 0.8 slice.148
  7.9 0.8 slice.150
  8.8 0.9 reshape.255
  9.7 1.4 fusion.22
  11.1 0.8 multiply_cosine_fusion
  11.9 0.7 compare_and_fusion.1
  13.9 1.3 fusion.9
  15.2 1.3 multiply_reduce_fusion.5
  16.5 53.7 %gather_weights.1 = (bf16[4,2,2,2,16,1536]{5,4,3,2,1,0:T(8,128)(2,1)S(1)}, bf16[4,2,2,2,16,1536]{5,4,3,2,1,0:T(8,128)(2,1)S(1)}, bf16[4,2,2,2,16,1536]{5,4,3,2,1...) custom-call(bf16[16,1536]{1,0:T(8,128)(2,1)S(1)} %copy-done.6, bf16[16,1536]{1,0:T(8,128)(2,1)S(1)} %slice.149.refs_1_, ...), custom_call_target="tpu_custom_call" | custom-call | tf_op jit(solution)/shard_map/gather_weights/pallas_call | solution.py:490
  70.2 1.2 copy-done.4
  71.4 1.5 copy-done.3
  73.1 1.3 fusion.72
  75.0 2.0 slice.194
  77.0 3.0 %slice.208 = bf16[32,48,576]{2,1,0:T(8,128)(2,1)} slice(bf16[32,64,640]{2,1,0:T(8,128)(2,1)} %bitcast.146), slice={[0:32], [16:64], [0:576]} | slice | bytes 3538944 | tf_op jit(solution)/shard_map/slice | solution.py:597
  80.1 2.2 %reshape.259 = bf16[64,4608]{1,0:T(8,128)(2,1)} reshape(bf16[32,16,576]{2,1,0:T(8,128)(2,1)} %slice.194) | data formatting | bytes 1179648 | tf_op jit(solution)/shard_map/reshape | solution.py:593
  82.3 1.9 fusion.69
  84.2 1.9 fusion.66
  86.2 0.7 slice.285
  87.0 0.8 subtract_convert_fusion.1
  87.8 0.6 subtract_convert_fusion.3
  88.4 3.9 %fusion.71 = (f32[3,3,256]{2,1,0:T(4,128)}, f32[3,3,256,256]{2,3,1,0:T(8,128)}) fusion(pred[256,256]{0,1:T(8,128)(4,1)} %compare_and_fusion.1, bf16[256,3,3,32]{0,3,2,1:T(8,128)(2,1)} %bitcast.161, bf16[256,3,3,32]{0,3,2,1:T(8,128)(2,1)} %bitcast.157, bf16[256,3,32]{0,2,1:T(8,128)(2,1)} %get-tuple-element.45, bf16[256,3,32]{0,2,1:T(8,128)(2,1)S(1)} %get-tuple-element.44), kind=kOutput, calls=%fused_computation.158 | convolution fusion | flops 78643456 | bytes 2827264 | tf_op jit(solution)/shard_map/sub | solution.py:637
  92.3 2.9 %convolution_convert_fusion.6 = bf16[3,64,3,256]{3,1,2,0:T(8,128)(2,1)} fusion(bf16[256,3,64,1]{0,2,3,1:T(8,128)(2,1)} %bitcast.170, f32[3,3,256]{2,1,0:T(4,128)} %get-tuple-element.55, pred[256,256]{0,1:T(8,128)(4,1)} %compare_and_fusion.1, bf16[256,3,3,32]{0,3,2,1:T(8,128)(2,1)} %bitcast.162, bf16[256,3,3,32]{0,3,2,1:T(8,128)(2,1)} %bitcast.158, ...), kind=kOutput, calls=%fused_computation.39 | convolution fusion | flops 154880512 | bytes 861184 | tf_op jit(solution)/shard_map/kgqt,tkd->qkgd/dot_general | solution.py:641
  95.2 1.7 convolution_convert_fusion.10
  96.9 2.2 %multiply_reduce_fusion.4 = (f32[256]{0:T(256)S(1)}, f32[256,576]{0,1:T(8,128)S(1)}) fusion(f32[256,576]{0,1:T(8,128)} %get-tuple-element.54, bf16[256,576]{0,1:T(8,128)(2,1)S(1)} %convolution_convert_fusion.10, bf16[64,1536]{1,0:T(8,128)(2,1)} %copy-done.33, bf16[512,1536]{1,0:T(8,128)(2,1)S(1)} %bitcast.138), kind=kOutput, calls=%fused_computation.73 | convolution fusion | flops 171638528 | bytes 3245056 | tf_op jit(solution)/shard_map/dot_general | solution.py:552
  99.1 0.8 copy-done.23
  100.7 0.8 fusion.19
  101.5 0.7 copy-done.5
  102.2 0.8 fusion.21
  103.2 0.7 copy-done.32
  103.9 2.8 %multiply_convert_fusion = (bf16[256,1536]{1,0:T(8,128)(2,1)}, bf16[256,1536]{1,0:T(8,128)(2,1)}, bf16[256,1536]{1,0:T(8,128)(2,1)}) fusion(f32[256,1536]{1,0:T(8,128)S(1)} %fusion.21, f32[256,1536]{1,0:T(8,128)S(1)} %fusion.19, bf16[1536,576]{1,0:T(8,128)(2,1)S(1)} %bitcast.155, f32[256,576]{0,1:T(8,128)S(1)} %copy-done.29), kind=kOutput, calls=%fused_computation.22 | convolution fusion | flops 459030528 | bytes 7864320 | tf_op jit(solution)/shard_map/dot_general | solution.py:552
  106.7 4.3 %convolution_convert_fusion.8 = bf16[256,576]{0,1:T(8,128)(2,1)} fusion(bf16[576,576]{1,0:T(8,128)(2,1)} %constant.34.clone, f32[256,576]{0,1:T(8,128)} %copy-done.23, bf16[256,1536]{1,0:T(8,128)(2,1)} %get-tuple-element.34, bf16[1536,576]{1,0:T(8,128)(2,1)} %bitcast.154, f32[256]{0:T(256)} %copy-done.69), kind=kOutput, calls=%fused_computation.41 | convolution fusion | flops 623443968 | bytes 4105216 | tf_op jit(solution)/shard_map/dot_general | solution.py:552
  111.0 2.5 %fusion.20 = f32[256,576]{0,1:T(8,128)S(1)} fusion(bf16[256,1536]{1,0:T(8,128)(2,1)} %get-tuple-element.33, bf16[64,1536]{1,0:T(8,128)(2,1)} %get-tuple-element.39, bf16[512,1536]{1,0:T(8,128)(2,1)} %bitcast.149), kind=kOutput, calls=%fused_computation.55 | convolution fusion | flops 456523776 | bytes 3145728 | tf_op jit(solution)/shard_map/dot_general | solution.py:552
  113.5 0.8 multiply_reduce_fusion
  115.5 1.8 convolution_convert_fusion.9
  117.2 2.9 %fusion.18 = bf16[3,64,256]{2,1,0:T(8,128)(2,1)} fusion(bf16[256,3,3,64]{0,3,2,1:T(8,128)(2,1)} %bitcast.165, f32[3,3,256]{2,1,0:T(4,128)} %get-tuple-element.55, pred[256,256]{0,1:T(8,128)(4,1)} %compare_and_fusion.1, bf16[256,3,3,32]{0,3,2,1:T(8,128)(2,1)} %bitcast.163, bf16[256,3,3,32]{0,3,2,1:T(8,128)(2,1)} %bitcast.159, ...), kind=kOutput, calls=%fused_computation.53 | convolution fusion | flops 154782208 | bytes 861184 | tf_op jit(solution)/shard_map/kgqt,qkgd->tkd/dot_general | solution.py:683
  120.2 3.0 %convolution_convert_fusion = bf16[1536,576]{0,1:T(8,128)(2,1)} fusion(bf16[256,1536]{1,0:T(8,128)(2,1)} %get-tuple-element.34, f32[256,576]{0,1:T(8,128)S(1)} %copy-done.31), kind=kOutput, calls=%fused_computation.3 | convolution fusion | flops 454017024 | bytes 3145728 | tf_op jit(solution)/shard_map/dot_general | solution.py:552
  123.2 4.0 %copy.33 = bf16[1536,576]{1,0:T(8,128)(2,1)} copy(bf16[1536,576]{0,1:T(8,128)(2,1)} %convolution_convert_fusion) | data formatting | bytes 3538944 | tf_op jit(solution)/shard_map/convert_element_type | solution.py:562
  127.2 1.3 convolution_convert_fusion.4
  129.3 1.1 copy-done.21
  131.7 1.3 slice.215
  133.4 1.1 copy-done.27
  139.2 1.3 convolution_convert_fusion.7
  140.6 1.7 convolution_convert_fusion.3
  142.4 0.9 fusion.25
  143.3 1.6 fusion.7
  144.9 1.7 reshape.273
  146.6 2.1 %fusion.2 = bf16[32,64,640]{2,1,0:T(8,128)(2,1)S(1)} fusion(bf16[32,1,36]{2,1,0:T(2,128)(2,1)S(1)} %reshape.289, bf16[32,48,576]{2,1,0:T(8,128)(2,1)} %bitcast.151, bf16[32,16,576]{2,1,0:T(8,128)(2,1)S(1)} %reshape.273), kind=kLoop, calls=%fused_computation.6 | loop fusion | flops 10485760 | bytes 4983040 | tf_op jit(solution)/shard_map/concatenate | solution.py:711
  149.0 48.3 %scatter_gradients.1 = (f32[16,1536]{1,0:T(8,128)S(1)}, f32[16,1536]{1,0:T(8,128)S(1)}, f32[16,1536]{1,0:T(8,128)S(1)}, f32[64,640]{1,0:T(8,128)S(1)}) custom-call(bf16[4,2,2,2,16,1536]{5,4,3,2,1,0:T(8,128)(2,1)S(1)} %bitcast.143, bf16[4,2,2,2,16,1536]{5,4,3,2,1,0:T(8,128)(2,1)S(1)} %bitcast.142, bf16[4,2,2,2,16,1536]{5,4,3,2,1,0:T(8,128)(2,1)S(1)} %bitcast.141, ...), custom_call_target="tpu_custom_call" | custom-call | tf_op jit(solution)/shard_map/scatter_gradients/pallas_call | solution.py:516
  199.2 0.7 fusion.42
  199.9 0.7 reshape.284
  200.9 0.7 reshape.280
  201.5 0.7 reshape.279
  202.2 0.7 fusion.47
  203.0 0.7 reshape.281
  203.7 0.7 reshape.278
  204.4 0.7 reshape.282
  205.1 0.7 reshape.283
  (191 shorter events, 14.0 us)
Async XLA Ops:
  0.6 14.5 %copy-start = (bf16[256,576]{0,1:T(8,128)(2,1)S(1)}, bf16[256,576]{0,1:T(8,128)(2,1)}, u32[]{:S(2)}) copy-start(bf16[256,576]{0,1:T(8,128)(2,1)} %param.12) | copy-start | bytes 884740
  0.7 11.2 %copy-start.58 = (s32[256]{0:T(256)S(1)}, s32[256]{0:T(256)}, u32[]{:S(2)}) copy-start(s32[256]{0:T(256)} %param.13) | copy-start | bytes 3076
  0.7 12.8 %copy-start.50 = (bf16[27648]{0:T(1024)(128)(2,1)S(1)}, bf16[27648]{0:T(1024)(128)(2,1)}, u32[]{:S(2)}) copy-start(bf16[27648]{0:T(1024)(128)(2,1)} %param.19) | copy-start | bytes 165892
  0.7 12.7 %copy-start.49 = (bf16[27648]{0:T(1024)(128)(2,1)S(1)}, bf16[27648]{0:T(1024)(128)(2,1)}, u32[]{:S(2)}) copy-start(bf16[27648]{0:T(1024)(128)(2,1)} %param.18) | copy-start | bytes 165892
  0.7 13.1 %copy-start.70 = (bf16[36]{0:T(256)(128)(2,1)S(1)}, bf16[36]{0:T(256)(128)(2,1)}, u32[]{:S(2)}) copy-start(bf16[36]{0:T(256)(128)(2,1)} %param.21) | copy-start | bytes 220
  1.4 12.4 %copy-start.69 = (f32[256]{0:T(256)}, f32[256]{0:T(256)S(1)}, u32[]{:S(2)}) copy-start(f32[256]{0:T(256)S(1)} %compare_convert_fusion) | copy-start | bytes 3076
  5.5 8.3 %copy-start.11 = (bf16[576,576]{1,0:T(8,128)(2,1)S(1)}, bf16[576,576]{1,0:T(8,128)(2,1)}, u32[]{:S(2)}) copy-start(bf16[576,576]{1,0:T(8,128)(2,1)} %constant.34.clone) | copy-start | bytes 1990660
  5.6 8.3 %copy-start.71 = (bf16[256,576]{0,1:T(8,128)(2,1)S(1)}, bf16[256,576]{0,1:T(8,128)(2,1)}, u32[]{:S(2)}) copy-start(bf16[256,576]{0,1:T(8,128)(2,1)} %param.22) | copy-start | bytes 884740
  13.9 2.6 %copy-start.6 = (bf16[16,1536]{1,0:T(8,128)(2,1)S(1)}, bf16[16,1536]{1,0:T(8,128)(2,1)}, u32[]{:S(2)}) copy-start(bf16[16,1536]{1,0:T(8,128)(2,1)} %slice.190.refs_0_) | copy-start | bytes 147460
  16.5 67.8 %copy-start.66 = (f32[256]{0:T(256)}, f32[256]{0:T(256)S(1)}, u32[]{:S(2)}) copy-start(f32[256]{0:T(256)S(1)} %add_rsqrt_fusion.1) | copy-start | bytes 3076
  70.2 1.2 copy-start.4
  71.4 1.5 copy-start.3
  75.0 9.2 %copy-start.59 = (f32[576]{0:T(1024)}, f32[576]{0:T(1024)S(1)}, u32[]{:S(2)}) copy-start(f32[576]{0:T(1024)S(1)} %get-tuple-element.31) | copy-start | bytes 6916
  84.2 2.0 copy-start.33
  96.9 2.3 %copy-start.25 = (bf16[256,576]{0,1:T(8,128)(2,1)}, bf16[256,576]{0,1:T(8,128)(2,1)S(1)}, u32[]{:S(2)}) copy-start(bf16[256,576]{0,1:T(8,128)(2,1)S(1)} %convolution_convert_fusion.10) | copy-start | bytes 884740
  96.9 3.6 %copy-start.56 = (f32[576]{0:T(1024)S(1)}, f32[576]{0:T(1024)}, u32[]{:S(2)}) copy-start(f32[576]{0:T(1024)} %get-tuple-element.30) | copy-start | bytes 6916
  96.9 3.7 %copy-start.38 = (bf16[64,1536]{1,0:T(8,128)(2,1)S(1)}, bf16[64,1536]{1,0:T(8,128)(2,1)}, u32[]{:S(2)}) copy-start(bf16[64,1536]{1,0:T(8,128)(2,1)} %get-tuple-element.40) | copy-start | bytes 589828
  100.6 1.5 copy-start.5
  100.7 1.5 copy-start.40
  102.2 1.7 copy-start.32
  110.9 2.5 %copy-start.24 = (f32[256,576]{0,1:T(8,128)S(1)}, f32[256,576]{0,1:T(8,128)}, u32[]{:S(2)}) copy-start(f32[256,576]{0,1:T(8,128)} %copy-done.23) | copy-start | bytes 1769476
  110.9 2.5 %copy-start.39 = (bf16[64,1536]{1,0:T(8,128)(2,1)S(1)}, bf16[64,1536]{1,0:T(8,128)(2,1)}, u32[]{:S(2)}) copy-start(bf16[64,1536]{1,0:T(8,128)(2,1)} %get-tuple-element.40) | copy-start | bytes 589828
  110.9 2.5 %copy-start.42 = (bf16[256,1536]{1,0:T(8,128)(2,1)S(1)}, bf16[256,1536]{1,0:T(8,128)(2,1)}, u32[]{:S(2)}) copy-start(bf16[256,1536]{1,0:T(8,128)(2,1)} %get-tuple-element.32) | copy-start | bytes 2359300
  111.0 2.5 %copy-start.57 = (f32[576]{0:T(1024)S(1)}, f32[576]{0:T(1024)}, u32[]{:S(2)}) copy-start(f32[576]{0:T(1024)} %get-tuple-element.30) | copy-start | bytes 6916
  111.0 2.5 %copy-start.65 = (f32[256]{0:T(256)S(1)}, f32[256]{0:T(256)}, u32[]{:S(2)}) copy-start(f32[256]{0:T(256)} %copy-done.64) | copy-start | bytes 3076
  113.5 1.4 copy-start.30
  114.3 1.2 copy-start.12
  114.3 1.2 copy-start.34
  115.5 11.7 %copy-start.15 = (f32[256,576]{0,1:T(8,128)}, f32[256,576]{0,1:T(8,128)S(1)}, u32[]{:S(2)}) copy-start(f32[256,576]{0,1:T(8,128)S(1)} %multiply_add_fusion) | copy-start | bytes 1769476
  115.5 1.8 copy-start.51
  117.2 3.0 %copy-start.31 = (f32[256,576]{0,1:T(8,128)S(1)}, f32[256,576]{0,1:T(8,128)}, u32[]{:S(2)}) copy-start(f32[256,576]{0,1:T(8,128)} %fusion.9) | copy-start | bytes 1769476
  123.2 4.0 %copy-start.26 = (bf16[256,576]{0,1:T(8,128)(2,1)S(1)}, bf16[256,576]{0,1:T(8,128)(2,1)}, u32[]{:S(2)}) copy-start(bf16[256,576]{0,1:T(8,128)(2,1)} %copy-done.25) | copy-start | bytes 884740
  123.2 5.3 %copy-start.18 = (bf16[256,576]{0,1:T(8,128)(2,1)S(1)}, bf16[256,576]{0,1:T(8,128)(2,1)}, u32[]{:S(2)}) copy-start(bf16[256,576]{0,1:T(8,128)(2,1)} %copy-done.17) | copy-start | bytes 884740
  127.2 1.3 copy-start.43
  129.2 1.3 copy-start.21
  129.2 1.3 copy-start.19
  129.2 1.9 copy-start.41
  131.6 1.8 copy-start.20
  131.7 2.9 %copy-start.27 = (f32[3,3,256,256]{2,3,1,0:T(8,128)S(1)}, f32[3,3,256,256]{2,3,1,0:T(8,128)}, u32[]{:S(2)}) copy-start(f32[3,3,256,256]{2,3,1,0:T(8,128)} %get-tuple-element.56) | copy-start | bytes 7077892
  131.7 2.9 %copy-start.46 = (bf16[256,576]{0,1:T(8,128)(2,1)S(1)}, bf16[256,576]{0,1:T(8,128)(2,1)}, u32[]{:S(2)}) copy-start(bf16[256,576]{0,1:T(8,128)(2,1)} %convolution_convert_fusion.9) | copy-start | bytes 884740
  131.7 2.9 %copy-start.53 = (bf16[256,192]{0,1:T(8,128)(2,1)S(1)}, bf16[256,192]{0,1:T(8,128)(2,1)}, u32[]{:S(2)}) copy-start(bf16[256,192]{0,1:T(8,128)(2,1)} %slice.285) | copy-start | bytes 294916
  131.7 2.9 %copy-start.62 = (f32[3,3,256]{2,1,0:T(4,128)S(1)}, f32[3,3,256]{2,1,0:T(4,128)}, u32[]{:S(2)}) copy-start(f32[3,3,256]{2,1,0:T(4,128)} %get-tuple-element.55) | copy-start | bytes 27652
  135.1 1.5 copy-start.52
  136.6 1.1 copy-start.35
  136.6 1.1 copy-start.60
  136.6 1.1 copy-start.72
  137.0 1.3 copy-start.54
  137.2 1.2 copy-start.47
  137.8 1.1 copy-start.13
  137.8 1.1 copy-start.63
  137.8 1.4 copy-start.16
  138.9 1.7 copy-start.48
  138.9 1.7 copy-start.55
  138.9 1.7 copy-start.61
  138.9 1.7 copy-start.68
  138.9 1.7 copy-start.73
  140.5 1.9 slice-start
  140.5 1.9 slice-start.1
  140.5 1.9 copy-start.22
  146.6 2.1 %copy-start.1 = (bf16[512,1536]{1,0:T(8,128)(2,1)S(1)}, bf16[512,1536]{1,0:T(8,128)(2,1)}, u32[]{:S(2)}) copy-start(bf16[512,1536]{1,0:T(8,128)(2,1)} %slice.215) | copy-start | bytes 4718596
  146.6 2.5 %copy-start.2 = (bf16[512,1536]{1,0:T(8,128)(2,1)S(1)}, bf16[512,1536]{1,0:T(8,128)(2,1)}, u32[]{:S(2)}) copy-start(bf16[512,1536]{1,0:T(8,128)(2,1)} %fusion.7) | copy-start | bytes 4718596
  149.0 50.1 %copy-start.14 = (bf16[576,576]{1,0:T(8,128)(2,1)S(1)}, bf16[576,576]{1,0:T(8,128)(2,1)}, u32[]{:S(2)}) copy-start(bf16[576,576]{1,0:T(8,128)(2,1)} %constant.34.clone) | copy-start | bytes 1990660
  198.6 5.8 %copy-start.8 = (f32[16,1536]{1,0:T(8,128)S(1)}, f32[16,1536]{1,0:T(8,128)}, u32[]{:S(2)}) copy-start(f32[16,1536]{1,0:T(8,128)} %copy-done.7) | copy-start | bytes 294916
  198.6 5.8 %copy-start.10 = (f32[16,1536]{1,0:T(8,128)S(1)}, f32[16,1536]{1,0:T(8,128)}, u32[]{:S(2)}) copy-start(f32[16,1536]{1,0:T(8,128)} %copy-done.9) | copy-start | bytes 294916
  (12 other events, 10.1 us)

commit v2 on v1

--- a/solution.py
+++ b/solution.py
@@ -536,16 +536,35 @@
 SPILL = ROWS - 16
 
 
-def order_matrix():
-    true_index = np.concatenate(
-        [
-            (np.arange(DEVICES)[:, None] * ROWS + np.arange(16)[None, :]).reshape(-1),
-            (np.arange(DEVICES)[:, None] * ROWS + 16 + np.arange(SPILL)[None, :]).reshape(-1),
-        ]
-    )
-    matrix = np.zeros((D, D), np.float32)
-    matrix[true_index, np.arange(D)] = 1.0
-    return matrix.astype(ml_dtypes.bfloat16)
+STREAM = 640
+CHUNK = 512
+PER_GAIN = 36
+
+
+def order_matrices():
+    main = (np.arange(DEVICES)[:, None] * ROWS + np.arange(16)[None, :]).reshape(-1)
+    spill = (np.arange(DEVICES)[:, None] * ROWS + 16 + np.arange(SPILL)[None, :]).reshape(-1)
+    stream = np.zeros((D, STREAM), np.float32)
+    stream[main, np.arange(512)] = 1.0
+    stream[spill, 576 + np.arange(64)] = 1.0
+    columns = np.concatenate([stream[:, 576:], stream[:, :512]], axis=1)
+    select = np.zeros((512, 512), np.float32)
+    for part in range(8):
+        for owner in range(DEVICES):
+            for row in range(SPILL):
+                select[part * 64 + owner * 2 + row, owner * 16 + row * 8 + part] = 1.0
+    true_index = np.full((STREAM,), -1)
+    true_index[:512] = main
+    true_index[576:] = spill
+    pick = np.zeros((2, 64, STREAM), np.float32)
+    holder = np.zeros((2, 64, STREAM), np.float32)
+    for half in range(2):
+        for lane in range(STREAM):
+            if true_index[lane] >= 0:
+                flat = half * D + true_index[lane]
+                pick[half, flat % PER_GAIN, lane] = 1.0
+                holder[half, 2 * (flat // PER_GAIN), lane] = 1.0
+    return tuple(value.astype(ml_dtypes.bfloat16) for value in (stream, columns, select, pick, holder))
 
 
 def dot(left, right, contract=(1, 0), precision=None):
@@ -562,176 +581,278 @@
     return dot(left, right, contract).astype(jnp.bfloat16)
 
 
+def swap_halves(values):
+    width = values.shape[1]
+    lane = lax.broadcasted_iota(jnp.int32, values.shape, 1)
+    return jnp.where(
+        lane % HEAD_DIM < HEAD_DIM // 2,
+        pltpu.roll(values, width - HEAD_DIM // 2, 1),
+        pltpu.roll(values, HEAD_DIM // 2, 1),
+    )
+
+
+def stream_norm(values):
+    root = lax.rsqrt(jnp.sum(values * values, axis=1, keepdims=True) * (1.0 / D) + NORM_EPSILON)
+    return values * root, root
+
+
+def stream_norm_back(grad_in, normed, root, gain_row):
+    scaled = grad_in * gain_row
+    mean = jnp.sum(scaled * normed, axis=1, keepdims=True) * (1.0 / D)
+    return root * (scaled - normed * mean)
+
+
+def layer_kernel(
+    tokens, cotangent, seg_row, seg_col, cosine, sine, stream, select, pick, holder,
+    mixed, gate, up, extra,
+    out_tokens, out_grad_tokens, g_mixed, g_gate, g_up, g_extra,
+    w_spill, w_down, g_spill, probs, heads, attended, g_heads, result, g_input,
+):
+    low = jnp.bfloat16
+    count = tokens.shape[0]
+    scale = HEAD_DIM ** (-0.5)
+    spill_in = extra[:, :16, :].reshape(512, STREAM)
+    spill_rows = low_dot(select[...], spill_in)
+    w_spill[0:64, :] = jnp.zeros((64, 8 * STREAM), low)
+    for part in range(8):
+        w_spill[64:128, part * STREAM : (part + 1) * STREAM] = spill_rows[part * 64 : part * 64 + 64]
+    w_down[...] = extra[:, 16:, :].reshape(FF, STREAM)
+    gain_block = spill_rows[448:512, 128:192]
+    gains = [
+        jnp.sum(dot(gain_block, pick[half]) * holder[half].astype(jnp.float32), axis=0, keepdims=True)
+        for half in range(2)
+    ]
+
+    values = dot(tokens[...], stream[...])
+    live = (seg_col[...] >= 0).astype(jnp.float32)
+    grad_result = dot(cotangent[...], stream[...]) * live
+    grad_down_in = grad_result.astype(low)
+    normed_one, root_one = stream_norm(values)
+    input_one = (normed_one * gains[0]).astype(low)
+    one_main, one_spill = input_one[:, :512], input_one[:, 512:]
+    qkv = dot(one_main, mixed[:, :1024]) + dot(one_spill, w_spill[:, :1024])
+    wide_cos = jnp.concatenate([cosine[...]] * 6, axis=1)
+    wide_sin = jnp.concatenate([sine[...]] * 6, axis=1)
+    turning = qkv[:, :768]
+    heads[:, :768] = (turning * wide_cos + swap_halves(turning) * wide_sin).astype(low)
+    heads[:, 768:] = qkv[:, 768:].astype(low)
+    column = lax.broadcasted_iota(jnp.int32, (count, count), 1)
+    row = lax.broadcasted_iota(jnp.int32, (count, count), 0)
+    allowed = (seg_col[...] == seg_row[...]) & (column <= row)
+
+    def head(array, start):
+        return array[:, start : start + HEAD_DIM]
+
+    for h in range(HEADS):
+        c = h // 3
+        scores = dot(head(heads, 64 * h), head(heads, 576 + 64 * c), (1, 1)) * scale
+        scores = jnp.where(allowed, scores, NEG_LARGE)
+        peak = jnp.max(scores, axis=1, keepdims=True)
+        powers = jnp.exp(scores - peak)
+        p = powers / jnp.sum(powers, axis=1, keepdims=True)
+        probs[h] = p
+        attended[:, 64 * h : 64 * h + 64] = low_dot(p.astype(low), head(heads, 768 + 64 * c))
+    att = low_dot(attended[...], stream[...])
+    att_main, att_spill = att[:, :512], att[:, 512:]
+    branch_main = dot(att_main, mixed[:, 1024:]) + dot(att_spill, w_spill[:, 1024:1536])
+    branch_spill = dot(att_main, mixed[:, 896:1024]) + dot(att_spill, w_spill[:, 896:1024])
+    lane = lax.broadcasted_iota(jnp.int32, branch_spill.shape, 1)
+    branch_spill = jnp.where(lane >= 64, branch_spill, 0.0)
+    middle = values + jnp.concatenate([branch_main, branch_spill], axis=1)
+    normed_two, root_two = stream_norm(middle)
+    input_two = (normed_two * gains[1]).astype(low)
+    two_main, two_spill = input_two[:, :512], input_two[:, 512:]
+    result[...] = middle
+    g_input[...] = jnp.zeros_like(g_input)
+
+    for start in range(0, FF, CHUNK):
+        here = slice(start, start + CHUNK)
+        gate_at = slice(FF + start, FF + start + CHUNK)
+        up_at = slice(2 * FF + start, 2 * FF + start + CHUNK)
+        gate_pre = dot(two_main, gate[:, here]) + dot(two_spill, w_spill[:, gate_at])
+        up_pre = dot(two_main, up[:, here]) + dot(two_spill, w_spill[:, up_at])
+        sig = 1.0 / (1.0 + jnp.exp(-gate_pre))
+        silu = gate_pre * sig
+        product = (silu * up_pre).astype(low)
+        down = w_down[here, :]
+        result[...] += dot(product, down)
+        w_down_grad = low_dot(product, grad_down_in, (0, 0))
+        g_product = dot(grad_down_in, down, (1, 1))
+        gg = (g_product * up_pre * sig * (1.0 + gate_pre * (1.0 - sig))).astype(low)
+        gu = (g_product * silu).astype(low)
+        g_input[:, :512] += dot(gg, gate[:, here], (1, 1)) + dot(gu, up[:, here], (1, 1))
+        g_input[:, 512:] += dot(gg, w_spill[:, gate_at], (1, 1)) + dot(gu, w_spill[:, up_at], (1, 1))
+        g_gate[:, here] = low_dot(two_main, gg, (0, 0))
+        g_up[:, here] = low_dot(two_main, gu, (0, 0))
+        g_spill[:, gate_at] = low_dot(two_spill, gg, (0, 0))[64:]
+        g_spill[:, up_at] = low_dot(two_spill, gu, (0, 0))[64:]
+        w_down[here, :] = w_down_grad
+    g_extra[:, 16:, :] = w_down[...].reshape(DEVICES, DOWN_ROWS, STREAM)
+    out_tokens[...] = low_dot((result[...] * live).astype(low), stream[...], (1, 1))
+
+    grad_input_two = g_input[...]
+    gain_grads = [None, jnp.sum(grad_input_two * normed_two, axis=0, keepdims=True)]
+    grad_middle = grad_result + stream_norm_back(grad_input_two, normed_two, root_two, gains[1])
+    grad_branch = grad_middle.astype(low)
+    branch_main, branch_spill = grad_branch[:, :512], grad_branch[:, 512:]
+    g_mixed[:, 1024:] = low_dot(att_main, branch_main, (0, 0))
+    g_spill[:, 1024:1536] = low_dot(att_spill, branch_main, (0, 0))[64:]
+    g_att = jnp.concatenate(
+        [
+            dot(branch_main, mixed[:, 1024:], (1, 1)) + dot(branch_spill, mixed[:, 896:1024], (1, 1)),
+            dot(branch_main, w_spill[:, 1024:1536], (1, 1))
+            + dot(branch_spill, w_spill[:, 896:1024], (1, 1)),
+        ],
+        axis=1,
+    )
+    attended[...] = low_dot(g_att.astype(low), stream[...], (1, 1))
+    g_heads[:, 896:] = jnp.zeros((count, 128), jnp.float32)
+    for c in range(KV_HEADS):
+        keys, vals = head(heads, 576 + 64 * c), head(heads, 768 + 64 * c)
+        g_keys, g_vals = 0.0, 0.0
+        for h in range(3 * c, 3 * c + 3):
+            p, g_a, q = probs[h], head(attended, 64 * h), head(heads, 64 * h)
+            gp = dot(g_a, vals, (1, 1))
+            centre = jnp.sum(p * gp, axis=1, keepdims=True)
+            gs = (p * (gp - centre)).astype(low)
+            g_heads[:, 64 * h : 64 * h + 64] = dot(gs, keys) * scale
+            g_keys = g_keys + dot(gs, q, (0, 0))
+            g_vals = g_vals + dot(p.astype(low), g_a, (0, 0))
+        g_heads[:, 576 + 64 * c : 640 + 64 * c] = g_keys * scale
+        g_heads[:, 768 + 64 * c : 832 + 64 * c] = g_vals
+    turning = g_heads[:, :768]
+    grad_qkv = jnp.concatenate(
+        [turning * wide_cos - swap_halves(turning) * wide_sin, g_heads[:, 768:]], axis=1
+    ).astype(low)
+    g_mixed[:, :896] = low_dot(one_main, grad_qkv[:, :896], (0, 0))
+    g_spill[:, :896] = low_dot(one_spill, grad_qkv[:, :896], (0, 0))[64:]
+    tail = grad_qkv[:, 896:]
+    g_mixed[:, 896:1024] = (dot(one_main, tail, (0, 0)) + dot(att_main, branch_spill, (0, 0))).astype(low)
+    g_spill[:, 896:1024] = (dot(one_spill, tail, (0, 0)) + dot(att_spill, branch_spill, (0, 0))).astype(low)[64:]
+    grad_input_one = jnp.concatenate(
+        [dot(grad_qkv, mixed[:, :1024], (1, 1)), dot(grad_qkv, w_spill[:, :1024], (1, 1))], axis=1
+    )
+    gain_grads[0] = jnp.sum(grad_input_one * normed_one, axis=0, keepdims=True)
+    grad_tokens = grad_middle + stream_norm_back(grad_input_one, normed_one, root_one, gains[0])
+    out_grad_tokens[...] = low_dot(grad_tokens.astype(low), stream[...], (1, 1))
+    block = 0.0
+    for half in range(2):
+        spread = holder[half].astype(jnp.float32) * gain_grads[half]
+        block = block + dot(spread.astype(low), pick[half], (1, 1))
+    g_spill[:, 3 * FF :] = jnp.concatenate(
+        [block, jnp.zeros((64, 8 * STREAM - 3 * FF - 64), jnp.float32)], axis=1
+    ).astype(low)
+    stacked = jnp.concatenate(
+        [g_spill[:, part * STREAM : (part + 1) * STREAM] for part in range(8)], axis=0
+    )
+    g_extra[:, :16, :] = low_dot(select[...], stacked, (0, 0)).reshape(DEVICES, 16, STREAM)
+
+
+def local_layer(*operands):
+    count = operands[0].shape[0]
+    low = jnp.bfloat16
+    vmem = pl.BlockSpec(memory_space=pltpu.VMEM)
+    return pl.pallas_call(
+        layer_kernel,
+        out_shape=(
+            jax.ShapeDtypeStruct((count, D), low),
+            jax.ShapeDtypeStruct((count, D), low),
+            jax.ShapeDtypeStruct((512, WIDE), low),
+            jax.ShapeDtypeStruct((512, WIDE), low),
+            jax.ShapeDtypeStruct((512, WIDE), low),
+            jax.ShapeDtypeStruct((DEVICES, 64, STREAM), low),
+        ),
+        in_specs=[vmem] * len(operands),
+        out_specs=(vmem,) * 6,
+        scratch_shapes=[
+            pltpu.VMEM((128, 8 * STREAM), low),
+            pltpu.VMEM((FF, STREAM), low),
+            pltpu.VMEM((64, 8 * STREAM), low),
+            pltpu.VMEM((HEADS, count, count), jnp.float32),
+            pltpu.VMEM((count, 1024), low),
+            pltpu.VMEM((count, D), low),
+            pltpu.VMEM((count, 1024), jnp.float32),
+            pltpu.VMEM((count, STREAM), jnp.float32),
+            pltpu.VMEM((count, STREAM), jnp.float32),
+        ],
+        compiler_params=pltpu.CompilerParams(vmem_limit_bytes=52 * 1024 * 1024),
+        name="local_layer",
+    )(*operands)
+
+
 def packed_device(
     tokens, segments, w_query, w_key, w_value, w_output, w_gate, w_up, w_down, gains, cotangent
 ):
     token_count = tokens.shape[0]
-    group_size = HEADS // KV_HEADS
-    score_scale = HEAD_DIM ** (-0.5)
-    order = jnp.asarray(order_matrix())
+    stream, columns, select, pick, holder = (jnp.asarray(value) for value in order_matrices())
+    share = gains.shape[0]
     rows = jnp.concatenate(
         [
             w_query.reshape(ROWS, D),
             w_key.reshape(ROWS, KV),
             w_value.reshape(ROWS, KV),
-            low_dot(w_output.reshape(ROWS, D), order),
+            low_dot(w_output.reshape(ROWS, D), columns),
             w_gate.reshape(ROWS, FF),
             w_up.reshape(ROWS, FF),
         ],
         axis=1,
     )
-    down_rows = low_dot(w_down.reshape(DOWN_ROWS, D), order)
-    share = gains.shape[0]
-    spare = jnp.pad(gains.reshape(1, share), ((0, 63), (0, 64 - share)))
-    extra = jnp.concatenate(
-        [jnp.concatenate([rows[16:].reshape(16, D), down_rows], axis=0), spare], axis=1
-    )
-    mixed, gate_part, up_part, extra_all = gather_packed(
-        (rows[:16, :WIDE], rows[:16, WIDE : 2 * WIDE], rows[:16, 2 * WIDE :], extra)
-    )
-    extra_all = extra_all.reshape(DEVICES, 64, NARROW)
-    spill = extra_all[:, :16, :D].reshape(DEVICES * SPILL, 3 * WIDE)
-    mixed = jnp.concatenate([mixed.reshape(512, WIDE), spill[:, :WIDE]], axis=0)
-    gate_matrix = jnp.concatenate([gate_part.reshape(512, WIDE), spill[:, WIDE : 2 * WIDE]], axis=0)
-    up_matrix = jnp.concatenate([up_part.reshape(512, WIDE), spill[:, 2 * WIDE :]], axis=0)
-    down_matrix = extra_all[:, 16:, :D].reshape(FF, D)
-    gain_all = extra_all[:, 0, D : D + share].reshape(2, D)
-    gain_rows = dot(gain_all, order)
-    gain_first, gain_second = gain_rows[0:1], gain_rows[1:2]
-    qkv_matrix = mixed[:, : D + 2 * KV]
-    output_matrix = mixed[:, D + 2 * KV :]
-
+    down_rows = low_dot(w_down.reshape(DOWN_ROWS, D), stream)
+    spare = jnp.pad(gains.reshape(1, share), ((0, 1), (0, 8 * STREAM - 3 * FF - share)))
+    spill = jnp.concatenate([rows[16:], spare], axis=1).reshape(16, STREAM)
+    weights = gather_packed(
+        (
+            rows[:16, :WIDE],
+            rows[:16, WIDE : 2 * WIDE],
+            rows[:16, 2 * WIDE :],
+            jnp.concatenate([spill, down_rows], axis=0),
+        )
+    )
     column = jnp.arange(token_count)[None, :]
     row_index = jnp.arange(token_count)[:, None]
     same_segment = segments[:, None] == segments[None, :]
     positions = jnp.sum((same_segment & (column < row_index)).astype(jnp.int32), axis=1)
-    allowed = same_segment & (column <= row_index)
     frequency = ROPE_BASE ** (-(2.0 * jnp.arange(HEAD_DIM // 2).astype(jnp.float32)) / HEAD_DIM)
     angles = positions.astype(jnp.float32)[:, None] * frequency[None, :]
-    cosine = jnp.cos(angles)[:, None, :]
-    sine_table = jnp.sin(angles)[:, None, :]
-    live_rows = (segments >= 0).astype(jnp.float32)[:, None]
-
-    token_values = dot(tokens, order)
-    grad_result = dot(cotangent, order) * live_rows
-    grad_down_in = grad_result.astype(jnp.bfloat16)
-
-    normed_one, root_one = normalize_parts(token_values)
-    input_one = (normed_one * gain_first).astype(jnp.bfloat16)
-    qkv = dot(input_one, qkv_matrix)
-    query_pre, key_pre = qkv[:, :D], qkv[:, D : D + KV]
-    value_low = qkv[:, D + KV :].astype(jnp.bfloat16).reshape(token_count, KV_HEADS, HEAD_DIM)
-    query_low = rotate(query_pre.reshape(token_count, HEADS, HEAD_DIM), cosine, sine_table).astype(
-        jnp.bfloat16
-    )
-    query_low = query_low.reshape(token_count, KV_HEADS, group_size, HEAD_DIM)
-    key_low = rotate(key_pre.reshape(token_count, KV_HEADS, HEAD_DIM), cosine, sine_table).astype(
-        jnp.bfloat16
-    )
-    scores = (
-        jnp.einsum("qkgd,tkd->kgqt", query_low, key_low, preferred_element_type=jnp.float32)
-        * score_scale
-    )
-    scores = jnp.where(allowed, scores, NEG_LARGE)
-    row_peak = jnp.max(scores, axis=-1, keepdims=True)
-    exponentials = jnp.exp(scores - row_peak)
-    totals = jnp.sum(exponentials, axis=-1, keepdims=True)
-    probabilities = exponentials / totals
-    probs_low = probabilities.astype(jnp.bfloat16)
-    attended = jnp.einsum("kgqt,tkd->qkgd", probs_low, value_low, preferred_element_type=jnp.float32)
-    attended_low = low_dot(attended.astype(jnp.bfloat16).reshape(token_count, D), order)
-    middle = token_values + dot(attended_low, output_matrix)
-    normed_two, root_two = normalize_parts(middle)
-    input_two = (normed_two * gain_second).astype(jnp.bfloat16)
-    gate_pre = dot(input_two, gate_matrix)
-    up_pre = dot(input_two, up_matrix)
-    sigmoid_gate = jax.nn.sigmoid(gate_pre)
-    silu_gate = gate_pre * sigmoid_gate
-    product_low = (silu_gate * up_pre).astype(jnp.bfloat16)
-    result = middle + dot(product_low, down_matrix)
-    output_tokens = low_dot((result * live_rows).astype(jnp.bfloat16), order, (1, 1))
-
-    grad_down = low_dot(product_low, grad_down_in, (0, 0))
-    grad_product = dot(grad_down_in, down_matrix, (1, 1))
-    grad_gate_pre = (
-        grad_product * up_pre * sigmoid_gate * (1.0 + gate_pre * (1.0 - sigmoid_gate))
-    ).astype(jnp.bfloat16)
-    grad_up_pre = (grad_product * silu_gate).astype(jnp.bfloat16)
-    grad_gate = low_dot(input_two, grad_gate_pre, (0, 0))
-    grad_up = low_dot(input_two, grad_up_pre, (0, 0))
-    grad_input_two = dot(grad_gate_pre, gate_matrix, (1, 1)) + dot(grad_up_pre, up_matrix, (1, 1))
-    grad_gain_two = jnp.sum(grad_input_two * normed_two, axis=0)
-    grad_middle = grad_result + norm_backward(grad_input_two, normed_two, root_two, gain_second)
-    grad_branch = grad_middle.astype(jnp.bfloat16)
-    grad_output = low_dot(attended_low, grad_branch, (0, 0))
-    grad_attended = low_dot(low_dot(grad_branch, output_matrix, (1, 1)), order, (1, 1))
-    grad_attended = grad_attended.reshape(token_count, KV_HEADS, group_size, HEAD_DIM)
-
-    grad_probs = jnp.einsum(
-        "qkgd,tkd->kgqt", grad_attended, value_low, preferred_element_type=jnp.float32
-    )
-    centre = jnp.sum(probabilities * grad_probs, axis=-1, keepdims=True)
-    grad_scores = (probabilities * (grad_probs - centre)).astype(jnp.bfloat16)
-    grad_queries = (
-        jnp.einsum("kgqt,tkd->qkgd", grad_scores, key_low, preferred_element_type=jnp.float32)
-        * score_scale
-    )
-    grad_keys = (
-        jnp.einsum("kgqt,qkgd->tkd", grad_scores, query_low, preferred_element_type=jnp.float32)
-        * score_scale
-    )
-    grad_values = jnp.einsum(
-        "kgqt,qkgd->tkd", probs_low, grad_attended, preferred_element_type=jnp.float32
-    )
-    grad_query_low = rotate_back(
-        grad_queries.reshape(token_count, HEADS, HEAD_DIM), cosine, sine_table
-    )
-    grad_qkv = jnp.concatenate(
-        [
-            grad_query_low.astype(jnp.bfloat16).reshape(token_count, D),
-            rotate_back(grad_keys, cosine, sine_table).astype(jnp.bfloat16).reshape(token_count, KV),
-            grad_values.astype(jnp.bfloat16).reshape(token_count, KV),
-        ],
-        axis=1,
-    )
-    grad_mixed = jnp.concatenate([low_dot(input_one, grad_qkv, (0, 0)), grad_output], axis=1)
-    grad_input_one = dot(grad_qkv, qkv_matrix, (1, 1))
-    grad_gain_one = jnp.sum(grad_input_one * normed_one, axis=0)
-    grad_tokens = grad_middle + norm_backward(grad_input_one, normed_one, root_one, gain_first)
-    grad_tokens = low_dot(grad_tokens.astype(jnp.bfloat16), order, (1, 1))
-
-    grad_gains = low_dot(jnp.stack([grad_gain_one, grad_gain_two]).astype(jnp.bfloat16), order, (1, 1))
-    grad_gains = jnp.pad(
-        grad_gains.reshape(DEVICES, 1, share), ((0, 0), (0, 63), (0, 64 - share))
-    )
-    spill = jnp.concatenate([grad_mixed[512:], grad_gate[512:], grad_up[512:]], axis=1)
-    extra = jnp.concatenate(
-        [spill.reshape(DEVICES, 16, D), grad_down.reshape(DEVICES, DOWN_ROWS, D)], axis=1
-    )
-    extra = jnp.concatenate([extra, grad_gains], axis=2)
+    cosine, sine = jnp.cos(angles), jnp.sin(angles)
+    output_tokens, grad_tokens, g_mixed, g_gate, g_up, g_extra = local_layer(
+        tokens,
+        cotangent,
+        segments[None, :],
+        segments[:, None],
+        jnp.concatenate([cosine] * 4, axis=1),
+        jnp.concatenate([-sine, sine, -sine, sine], axis=1),
+        stream,
+        select,
+        pick,
+        holder,
+        weights[0].reshape(512, WIDE),
+        weights[1].reshape(512, WIDE),
+        weights[2].reshape(512, WIDE),
+        weights[3].reshape(DEVICES, 64, STREAM),
+    )
     mixed, gate_part, up_part, extra = scatter_packed(
         (
-            grad_mixed[:512].reshape(AXIS_SIZES + SHAPES[0]),
-            grad_gate[:512].reshape(AXIS_SIZES + SHAPES[1]),
-            grad_up[:512].reshape(AXIS_SIZES + SHAPES[2]),
-            extra.reshape(AXIS_SIZES + SHAPES[3]),
+            g_mixed.reshape(AXIS_SIZES + SHAPES[0]),
+            g_gate.reshape(AXIS_SIZES + SHAPES[1]),
+            g_up.reshape(AXIS_SIZES + SHAPES[2]),
+            g_extra.reshape(AXIS_SIZES + SHAPES[3]),
         )
     )
-    spill = extra[:16, :D].reshape(SPILL, 3 * WIDE)
+    spill = extra[:16].reshape(SPILL, 8 * STREAM)
     mixed = jnp.concatenate([mixed, spill[:, :WIDE]], axis=0)
     exact = lax.Precision.HIGHEST
-    wide_order = order.astype(jnp.float32)
     return (
         output_tokens,
         grad_tokens,
         mixed[:, :D].reshape(-1),
         mixed[:, D : D + KV].reshape(-1),
         mixed[:, D + KV : D + 2 * KV].reshape(-1),
-        dot(mixed[:, D + 2 * KV :], wide_order, (1, 1), exact).reshape(-1),
+        dot(mixed[:, D + 2 * KV :], columns.astype(jnp.float32), (1, 1), exact).reshape(-1),
         jnp.concatenate([gate_part, spill[:, WIDE : 2 * WIDE]], axis=0).reshape(-1),
-        jnp.concatenate([up_part, spill[:, 2 * WIDE :]], axis=0).reshape(-1),
-        dot(extra[16:, :D], wide_order, (1, 1), exact).reshape(-1),
-        extra[0, D : D + share],
+        jnp.concatenate([up_part, spill[:, 2 * WIDE : 3 * WIDE]], axis=0).reshape(-1),
+        dot(extra[16:], stream.astype(jnp.float32), (1, 1), exact).reshape(-1),
+        extra[7, 128 : 128 + share],
     )
 
 

time: 207 us -> 158 us (0.76)
  matrix products: 48.1 us -> 3.07 us
  Pallas kernels: 102 us -> 126 us
  local copies, waits for them, and re-layouts: 43.9 us -> 25.9 us
  other arithmetic: 10.2 us -> 1.9 us
    dot_general x25 -> x4, matrix products: 37 us -> 3.07 us  [dot(): lax.dot_general(left, right, (((contract[0],), (contract[1],)), ((), ()))...]
    pallas_call x0 -> x1, Pallas kernels: none -> 23.8 us  [local_layer(): pl.pallas_call(layer_kernel, out_shape=(jax.ShapeDtypeStruct((count, D),...]
    slice x17 -> x3, local copies, waits for them, and re-layouts: 9.84 us -> 0.02 us  [the longest x1 0.01 us: packed_device(): spill = jnp.concatenate([rows[16:], spare], axis=1).reshape(16, STREAM)]
    dot_general x5 -> x0, matrix products: 7.21 us -> none  [the longest x1 2.95 us: packed_device(): jnp.einsum('kgqt,qkgd->tkd', probs_low, grad_attended, preferred_element_...]
    concatenate x6 -> x4, other arithmetic: 4.65 us -> 0.32 us  [the longest x1 0.27 us: packed_device(): jnp.concatenate([cosine] * 4, axis=1)]
    reshape x9 -> x6, local copies, waits for them, and re-layouts: 7.25 us -> 3.08 us  [the longest x1 0.92 us: packed_device(): down_rows = low_dot(w_down.reshape(DOWN_ROWS, D), stream)]
    convert_element_type x1 -> x0, local copies, waits for them, and re-layouts: 3.96 us -> none  [low_dot(): return dot(left, right, contract).astype(jnp.bfloat16)]
    sub x1 -> x0, matrix products: 3.9 us -> none  [packed_device(): exponentials = jnp.exp(scores - row_peak)]
where the time goes in v2:
time: 158 us
  Pallas kernels  126 us (80%)
  local copies, waits for them, and re-layouts  25.9 us (16%)
  matrix products  3.07 us (2%)
  other arithmetic  1.9 us (1%)
    pallas_call x1, Pallas kernels, gather_packed(): pl.pallas_call(gather_kernel, out_shape=tuple((jax.ShapeDtypeStruct(AXIS_...  53.7 us
    pallas_call x1, Pallas kernels, scatter_packed(): pl.pallas_call(scatter_kernel, out_shape=tuple((jax.ShapeDtypeStruct(shap...  48.4 us
    pallas_call x1, Pallas kernels, local_layer(): pl.pallas_call(layer_kernel, out_shape=(jax.ShapeDtypeStruct((count, D),...  23.8 us
    unnamed x42, local copies, waits for them, and re-layouts  13.9 us

profile of v2, /device:TPU:0, one launch (start us, length us, event | category | flops | bytes accessed | tf_op | source)
XLA Modules:
  0.0 157.7 jit_solution(6459016840415033583)
XLA Ops:
  0.6 0.0 copy-start.11
  0.7 0.0 copy-start.17
  0.7 0.0 copy-start.16
  0.7 0.9 convert_reduce_fusion
  1.6 0.8 reshape.127
  2.4 0.8 reshape.128
  3.2 0.8 reshape.126
  4.0 0.8 reshape.129
  4.9 0.0 copy-start.18
  4.9 0.0 copy-start.10
  4.9 1.3 fusion.1
  6.2 0.0 copy-start.14
  6.2 0.8 slice.66
  7.1 0.1 slice.67.refs_1_
  7.2 0.0 copy-start.15
  7.2 0.8 slice.68
  8.0 0.1 slice.69.refs_2_
  8.1 0.9 reshape.134
  9.1 0.0 copy-done.11
  9.1 0.2 fusion
  9.3 0.1 concatenate.29
  9.4 0.0 copy-done.16
  9.5 0.1 reshape.130
  9.6 0.0 copy-done.17
  9.6 0.1 reshape.131
  9.7 0.1 concatenate.30
  9.8 0.0 copy-start.8
  9.8 0.0 copy-start.9
  9.8 0.0 copy-done.18
  9.9 0.1 copy.43.seg_col
  10.1 0.2 copy.41.tokens
  10.3 0.0 copy-done.15
  10.3 0.9 copy.42.cotangent
  11.2 0.5 fusion.7
  11.7 0.3 pad_maximum_fusion.2
  12.0 53.7 %gather_weights.1 = (bf16[4,2,2,2,16,1536]{5,4,3,2,1,0:T(8,128)(2,1)S(1)}, bf16[4,2,2,2,16,1536]{5,4,3,2,1,0:T(8,128)(2,1)S(1)}, bf16[4,2,2,2,16,1536]{5,4,3,2,1...) custom-call(bf16[16,1536]{1,0:T(8,128)(2,1)S(1)} %slice.81.refs_0_, bf16[16,1536]{1,0:T(8,128)(2,1)S(1)} %slice.67.refs_1_, ...), custom_call_target="tpu_custom_call" | custom-call | tf_op jit(solution)/shard_map/gather_weights/pallas_call | solution.py:490
  65.7 0.0 copy-start.1
  65.7 1.5 copy-done.1
  67.2 1.2 copy-done.5
  68.3 1.2 copy-done.6
  69.6 1.2 copy-done.7
  70.8 0.0 copy-done.9
  70.8 23.8 %local_layer.1 = (bf16[256,576]{1,0:T(8,128)(2,1)S(1)}, bf16[256,576]{1,0:T(8,128)(2,1)S(1)}, bf16[512,1536]{1,0:T(8,128)(2,1)}, bf16[512,1536]{1,0:T(8,128)(2,1...) custom-call(bf16[256,576]{1,0:T(8,128)(2,1)S(1)} %copy.41.tokens, bf16[256,576]{1,0:T(8,128)(2,1)} %copy.42.cotangent, ...), custom_call_target="tpu_custom_call" | custom-call | tf_op jit(solution)/shard_map/local_layer/pallas_call | solution.py:755
  94.6 0.9 copy.44
  95.4 0.9 copy.45
  96.3 1.7 %copy-done = bf16[32,64,640]{2,1,0:T(8,128)(2,1)S(1)} copy-done((bf16[32,64,640]{2,1,0:T(8,128)(2,1)S(1)}, bf16[32,64,640]{2,1,0:T(8,128)(2,1)}, u32[]{:S(2)}) %copy-start) | copy-done | bytes 2621464
  98.1 1.4 copy-done.2
  99.5 1.4 copy-done.3
  100.9 1.4 copy-done.4
  102.3 48.4 %scatter_gradients.1 = (f32[16,1536]{1,0:T(8,128)S(1)}, f32[16,1536]{1,0:T(8,128)S(1)}, f32[16,1536]{1,0:T(8,128)S(1)}, f32[64,640]{1,0:T(8,128)S(1)}) custom-call(bf16[4,2,2,2,16,1536]{5,4,3,2,1,0:T(8,128)(2,1)S(1)} %bitcast.25, bf16[4,2,2,2,16,1536]{5,4,3,2,1,0:T(8,128)(2,1)S(1)} %bitcast.26, bf16[4,2,2,2,16,1536]{5,4,3,2,1,0:T(8,128)(2,1)S(1)} %bitcast.27, ...), custom_call_target="tpu_custom_call" | custom-call | tf_op jit(solution)/shard_map/scatter_gradients/pallas_call | solution.py:516
  150.6 0.0 copy-start.13
  150.7 0.5 slice_bitcast_fusion
  151.2 0.0 copy-done.12
  151.2 0.7 fusion.3
  151.9 0.7 reshape.150
  152.7 0.7 reshape.149
  153.4 0.7 reshape.148
  154.1 0.1 fusion.8
  154.1 0.7 reshape.146
  154.8 0.7 reshape.145
  155.5 0.0 copy-done.13
  155.5 0.7 fusion.6
  156.2 0.7 reshape.147
  157.0 0.7 reshape.144
  (24 shorter events, 0.2 us)
Async XLA Ops:
  0.6 8.4 %copy-start.11 = (bf16[576,640]{1,0:T(8,128)(2,1)S(1)}, bf16[576,640]{1,0:T(8,128)(2,1)}, u32[]{:S(2)}) copy-start(bf16[576,640]{1,0:T(8,128)(2,1)} %constant.21.clone.stream) | copy-start | bytes 2211844
  0.7 8.9 %copy-start.17 = (bf16[27648]{0:T(1024)(128)(2,1)S(1)}, bf16[27648]{0:T(1024)(128)(2,1)}, u32[]{:S(2)}) copy-start(bf16[27648]{0:T(1024)(128)(2,1)} %param.23) | copy-start | bytes 165892
  0.7 8.8 %copy-start.16 = (bf16[27648]{0:T(1024)(128)(2,1)S(1)}, bf16[27648]{0:T(1024)(128)(2,1)}, u32[]{:S(2)}) copy-start(bf16[27648]{0:T(1024)(128)(2,1)} %param.22) | copy-start | bytes 165892
  4.9 4.9 %copy-start.18 = (bf16[36]{0:T(256)(128)(2,1)S(1)}, bf16[36]{0:T(256)(128)(2,1)}, u32[]{:S(2)}) copy-start(bf16[36]{0:T(256)(128)(2,1)} %param.25) | copy-start | bytes 220
  4.9 5.0 %copy-start.10 = (s32[256]{0:T(256)S(1)}, s32[256]{0:T(256)}, u32[]{:S(2)}) copy-start(s32[256]{0:T(256)} %param.17) | copy-start | bytes 3076
  6.2 3.8 %copy-start.14 = (bf16[256,576]{0,1:T(8,128)(2,1)S(1)}, bf16[256,576]{0,1:T(8,128)(2,1)}, u32[]{:S(2)}) copy-start(bf16[256,576]{0,1:T(8,128)(2,1)} %param.16) | copy-start | bytes 884740
  7.2 3.1 %copy-start.15 = (bf16[256,576]{0,1:T(8,128)(2,1)S(1)}, bf16[256,576]{0,1:T(8,128)(2,1)}, u32[]{:S(2)}) copy-start(bf16[256,576]{0,1:T(8,128)(2,1)} %param.26) | copy-start | bytes 884740
  9.8 61.0 %copy-start.8 = (bf16[2,64,640]{2,1,0:T(8,128)(2,1)S(1)}, bf16[2,64,640]{2,1,0:T(8,128)(2,1)}, u32[]{:S(2)}) copy-start(bf16[2,64,640]{2,1,0:T(8,128)(2,1)} %constant.25.clone.holder) | copy-start | bytes 491524
  9.8 61.0 %copy-start.9 = (bf16[2,64,640]{2,1,0:T(8,128)(2,1)S(1)}, bf16[2,64,640]{2,1,0:T(8,128)(2,1)}, u32[]{:S(2)}) copy-start(bf16[2,64,640]{2,1,0:T(8,128)(2,1)} %constant.24.clone.pick) | copy-start | bytes 491524
  65.7 1.5 copy-start.1
  67.2 1.2 copy-start.5
  68.3 1.2 copy-start.6
  69.5 1.2 copy-start.7
  96.3 1.7 %copy-start = (bf16[32,64,640]{2,1,0:T(8,128)(2,1)S(1)}, bf16[32,64,640]{2,1,0:T(8,128)(2,1)}, u32[]{:S(2)}) copy-start(bf16[32,64,640]{2,1,0:T(8,128)(2,1)} %get-tuple-element.33) | copy-start | bytes 7864324
  98.0 1.4 copy-start.2
  99.5 1.4 copy-start.3
  100.9 1.4 copy-start.4
  102.3 48.9 %copy-start.12 = (bf16[576,640]{1,0:T(8,128)(2,1)S(1)}, bf16[576,640]{1,0:T(8,128)(2,1)}, u32[]{:S(2)}) copy-start(bf16[576,640]{1,0:T(8,128)(2,1)} %constant.21.clone.stream) | copy-start | bytes 2211844
  150.6 4.9 %copy-start.13 = (bf16[576,576]{1,0:T(8,128)(2,1)S(1)}, bf16[576,576]{1,0:T(8,128)(2,1)}, u32[]{:S(2)}) copy-start(bf16[576,576]{1,0:T(8,128)(2,1)} %constant.22.clone) | copy-start | bytes 1990660

commit v3 on v2

--- a/solution.py
+++ b/solution.py
@@ -300,12 +300,25 @@
 
 
 AXIS_SIZES = (4, 2, 2, 2)
-ORDERS = ((1, 0, 2), (0, 2, 1), (2, 0, 1), (0, 1, 2))
 ARRAYS = 4
 WIDE = 1536
 NARROW = 640
 SHAPES = ((16, WIDE), (16, WIDE), (16, WIDE), (64, NARROW))
 MESH = pl.DeviceIdType.MESH
+PIECES = (
+    (0, 0, 16, 0, 768, (1, 0, 2)),
+    (0, 0, 16, 768, 768, (2, 0, 1)),
+    (1, 0, 16, 0, 768, (1, 0, 2)),
+    (1, 0, 16, 768, 768, (2, 0, 1)),
+    (2, 0, 16, 0, 768, (0, 1, 2)),
+    (2, 0, 16, 768, 768, (0, 2, 1)),
+    (3, 0, 32, 0, NARROW, (0, 1, 2)),
+    (3, 32, 32, 0, NARROW, (0, 2, 1)),
+)
+
+
+def window(piece):
+    return (pl.ds(piece[1], piece[2]), pl.ds(piece[3], piece[4]))
 
 
 def coordinates():
@@ -342,9 +355,11 @@
     coords = coordinates()
     enter(coords)
 
-    def run(which):
-        out = outs[which]
-        out[coords[0], coords[1], coords[2], coords[3]] = ins[which][...]
+    for which in range(ARRAYS):
+        outs[which][coords[0], coords[1], coords[2], coords[3]] = ins[which][...]
+
+    def run(which, piece):
+        out = outs[piece[0]]
         counter = [0]
         index = list(coords)
         sibling = peers_along(coords, 3)[0]
@@ -353,7 +368,7 @@
         def push(block, target):
             slot = counter[0]
             counter[0] += 1
-            view = out.at[tuple(block)]
+            view = out.at[tuple(block) + window(piece)]
             copy = pltpu.make_async_remote_copy(
                 src_ref=view,
                 dst_ref=view,
@@ -366,7 +381,7 @@
             return copy
 
         pending_core = [list(index)]
-        for dim in ORDERS[which]:
+        for dim in piece[5]:
             copies = [push(index, other) for other in peers_along(coords, dim)]
             for block in pending_core:
                 core_copies.append(push(block, sibling))
@@ -385,7 +400,7 @@
         for copy in core_copies:
             copy.wait()
 
-    drive([run(which) for which in range(ARRAYS)])
+    drive([run(which, piece) for which, piece in enumerate(PIECES)])
 
 
 def drive(tasks):
@@ -402,15 +417,15 @@
 
 def scatter_kernel(*refs):
     ins, outs = refs[:ARRAYS], refs[ARRAYS : 2 * ARRAYS]
-    landing = refs[2 * ARRAYS : 6 * ARRAYS]
-    send_sem, recv_sem = refs[6 * ARRAYS :]
+    landing = refs[2 * ARRAYS : -2]
+    send_sem, recv_sem = refs[-2:]
     coords = coordinates()
     enter(coords)
 
-    def run(which):
-        order = (3,) + tuple(reversed(ORDERS[which]))
+    def run(which, piece):
+        order = (3,) + tuple(reversed(piece[5]))
         remaining = [0, 1, 2, 3]
-        current = ins[which]
+        current = ins[piece[0]]
         counter = [0]
 
         def push(stage, dim, part, offset, target):
@@ -419,6 +434,8 @@
             index = tuple(
                 part if axis == dim else slice(None) for axis in remaining
             )
+            if stage == 0:
+                index = index + window(piece)
             land = landing[which * 4 + stage]
             copy = pltpu.make_async_remote_copy(
                 src_ref=current.at[index],
@@ -443,7 +460,7 @@
             rest = [axis for axis in remaining if axis != dim]
             last = stage == 3
 
-            def add_group(fixed, current=current, land=land, rest=rest, dim=dim, last=last, held=tuple(remaining)):
+            def add_group(fixed, current=current, land=land, rest=rest, dim=dim, last=last, held=tuple(remaining), first=stage == 0):
                 loose = [axis for axis in rest if axis not in fixed]
                 total = 1
                 for axis in loose:
@@ -457,11 +474,13 @@
                         left = left // AXIS_SIZES[axis]
                     mine = tuple(coords[dim] if axis == dim else at[axis] for axis in held)
                     target = tuple(at[axis] for axis in rest)
+                    if first:
+                        mine = mine + window(piece)
                     value = current[mine].astype(jnp.float32)
                     for offset in range(AXIS_SIZES[dim] - 1):
                         value = value + land[(offset,) + target].astype(jnp.float32)
                     if last:
-                        outs[which][...] = value
+                        outs[piece[0]][window(piece)] = value
                     else:
                         land[(0,) + target] = value.astype(jnp.bfloat16)
                     return carry
@@ -483,7 +502,7 @@
                 copies.append(push(stage + 1, following, other[following], offset, other))
             add_group({following: coords[following]})
 
-    drive([run(which) for which in range(ARRAYS)])
+    drive([run(which, piece) for which, piece in enumerate(PIECES)])
 
 
 def gather_packed(parts):
@@ -493,8 +512,8 @@
         in_specs=[pl.BlockSpec(memory_space=pltpu.VMEM)] * ARRAYS,
         out_specs=tuple([pl.BlockSpec(memory_space=pltpu.VMEM)] * ARRAYS),
         scratch_shapes=[
-            pltpu.SemaphoreType.DMA((ARRAYS, 12)),
-            pltpu.SemaphoreType.DMA((ARRAYS, 12)),
+            pltpu.SemaphoreType.DMA((len(PIECES), 12)),
+            pltpu.SemaphoreType.DMA((len(PIECES), 12)),
         ],
         compiler_params=pltpu.CompilerParams(
             collective_id=0, has_side_effects=True, vmem_limit_bytes=32 * 1024 * 1024
@@ -505,13 +524,13 @@
 
 def scatter_packed(parts):
     landing = []
-    for which in range(ARRAYS):
+    for piece in PIECES:
         remaining = [0, 1, 2, 3]
-        for dim in (3,) + tuple(reversed(ORDERS[which])):
+        for dim in (3,) + tuple(reversed(piece[5])):
             remaining = [axis for axis in remaining if axis != dim]
             extent = tuple(AXIS_SIZES[axis] for axis in remaining)
             landing.append(
-                pltpu.VMEM((AXIS_SIZES[dim] - 1,) + extent + SHAPES[which], jnp.bfloat16)
+                pltpu.VMEM((AXIS_SIZES[dim] - 1,) + extent + (piece[2], piece[4]), jnp.bfloat16)
             )
     return pl.pallas_call(
         scatter_kernel,
@@ -520,8 +539,8 @@
         out_specs=tuple([pl.BlockSpec(memory_space=pltpu.VMEM)] * ARRAYS),
         scratch_shapes=landing
         + [
-            pltpu.SemaphoreType.DMA((ARRAYS, 8)),
-            pltpu.SemaphoreType.DMA((ARRAYS, 8)),
+            pltpu.SemaphoreType.DMA((len(PIECES), 8)),
+            pltpu.SemaphoreType.DMA((len(PIECES), 8)),
         ],
         compiler_params=pltpu.CompilerParams(
             collective_id=1, has_side_effects=True, vmem_limit_bytes=40 * 1024 * 1024

time: 158 us -> 153 us (0.968)
  Pallas kernels: 126 us -> 120 us
    pallas_call x1, Pallas kernels: 48.4 us -> 43 us  [scatter_packed(): pl.pallas_call(scatter_kernel, out_shape=tuple((jax.ShapeDtypeStruct(shap...]
where the time goes in v3:
time: 153 us; the launch traced here: 152 us
  Pallas kernels  120 us (78%)
  local copies, waits for them, and re-layouts  25.9 us (17%)
  matrix products  3.07 us (2%)
  other arithmetic  1.9 us (1%)
    pallas_call x1, Pallas kernels, gather_packed(): pl.pallas_call(gather_kernel, out_shape=tuple((jax.ShapeDtypeStruct(AXIS_...  53.7 us
    pallas_call x1, Pallas kernels, scatter_packed(): pl.pallas_call(scatter_kernel, out_shape=tuple((jax.ShapeDtypeStruct(shap...  43 us
    pallas_call x1, Pallas kernels, local_layer(): pl.pallas_call(layer_kernel, out_shape=(jax.ShapeDtypeStruct((count, D),...  23.8 us
    unnamed x42, local copies, waits for them, and re-layouts  13.9 us
    dot_general x4, matrix products, dot(): lax.dot_general(left, right, (((contract[0],), (contract[1],)), ((), ()))...  3.07 us

profile of v3, /device:TPU:0, one launch (start us, length us, event | category | flops | bytes accessed | tf_op | source)
XLA Modules:
  0.0 152.2 jit_solution(12559814898920124298)
XLA Ops:
  0.6 0.0 copy-start.11
  0.7 0.0 copy-start.17
  0.7 0.0 copy-start.16
  0.7 0.9 convert_reduce_fusion
  1.6 0.8 reshape.127
  2.4 0.8 reshape.128
  3.2 0.8 reshape.126
  4.0 0.8 reshape.129
  4.9 0.0 copy-start.18
  4.9 0.0 copy-start.10
  4.9 1.3 fusion.1
  6.2 0.0 copy-start.14
  6.2 0.8 slice.66
  7.1 0.1 slice.67.refs_1_
  7.2 0.0 copy-start.15
  7.2 0.8 slice.68
  8.0 0.1 slice.69.refs_2_
  8.1 0.9 reshape.134
  9.1 0.0 copy-done.11
  9.1 0.2 fusion
  9.3 0.1 concatenate.29
  9.4 0.0 copy-done.16
  9.5 0.1 reshape.130
  9.6 0.0 copy-done.17
  9.6 0.1 reshape.131
  9.7 0.1 concatenate.30
  9.8 0.0 copy-start.8
  9.8 0.0 copy-start.9
  9.8 0.0 copy-done.18
  9.9 0.0 copy-done.10
  9.9 0.1 copy.43.seg_col
  10.0 0.0 copy-done.14
  10.1 0.2 copy.41.tokens
  10.3 0.0 copy-done.15
  10.3 0.9 copy.42.cotangent
  11.2 0.5 fusion.7
  11.7 0.3 pad_maximum_fusion.2
  12.0 53.7 %gather_weights.1 = (bf16[4,2,2,2,16,1536]{5,4,3,2,1,0:T(8,128)(2,1)S(1)}, bf16[4,2,2,2,16,1536]{5,4,3,2,1,0:T(8,128)(2,1)S(1)}, bf16[4,2,2,2,16,1536]{5,4,3,2,1...) custom-call(bf16[16,1536]{1,0:T(8,128)(2,1)S(1)} %slice.81.refs_0_, bf16[16,1536]{1,0:T(8,128)(2,1)S(1)} %slice.67.refs_1_, ...), custom_call_target="tpu_custom_call" | custom-call | tf_op jit(solution)/shard_map/gather_weights/pallas_call | solution.py:509
  65.7 0.0 copy-start.1
  65.7 1.5 copy-done.1
  67.2 1.2 copy-done.5
  68.3 1.2 copy-done.6
  69.5 1.2 copy-done.7
  70.7 23.8 %local_layer.1 = (bf16[256,576]{1,0:T(8,128)(2,1)S(1)}, bf16[256,576]{1,0:T(8,128)(2,1)S(1)}, bf16[512,1536]{1,0:T(8,128)(2,1)}, bf16[512,1536]{1,0:T(8,128)(2,1...) custom-call(bf16[256,576]{1,0:T(8,128)(2,1)S(1)} %copy.41.tokens, bf16[256,576]{1,0:T(8,128)(2,1)} %copy.42.cotangent, ...), custom_call_target="tpu_custom_call" | custom-call | tf_op jit(solution)/shard_map/local_layer/pallas_call | solution.py:774
  94.5 0.9 copy.44
  95.4 0.9 copy.45
  96.3 1.7 %copy-done = bf16[32,64,640]{2,1,0:T(8,128)(2,1)S(1)} copy-done((bf16[32,64,640]{2,1,0:T(8,128)(2,1)S(1)}, bf16[32,64,640]{2,1,0:T(8,128)(2,1)}, u32[]{:S(2)}) %copy-start) | copy-done | bytes 2621464
  98.0 1.4 copy-done.2
  99.4 1.4 copy-done.3
  100.8 1.4 copy-done.4
  102.2 43.0 %scatter_gradients.1 = (f32[16,1536]{1,0:T(8,128)S(1)}, f32[16,1536]{1,0:T(8,128)S(1)}, f32[16,1536]{1,0:T(8,128)S(1)}, f32[64,640]{1,0:T(8,128)S(1)}) custom-call(bf16[4,2,2,2,16,1536]{5,4,3,2,1,0:T(8,128)(2,1)S(1)} %bitcast.25, bf16[4,2,2,2,16,1536]{5,4,3,2,1,0:T(8,128)(2,1)S(1)} %bitcast.26, bf16[4,2,2,2,16,1536]{5,4,3,2,1,0:T(8,128)(2,1)S(1)} %bitcast.27, ...), custom_call_target="tpu_custom_call" | custom-call | tf_op jit(solution)/shard_map/scatter_gradients/pallas_call | solution.py:535
  145.2 0.0 copy-start.13
  145.2 0.5 slice_bitcast_fusion
  145.7 0.0 copy-done.12
  145.7 0.7 fusion.3
  146.5 0.7 reshape.150
  147.3 0.7 reshape.149
  148.0 0.7 reshape.148
  148.6 0.1 fusion.8
  148.7 0.7 reshape.146
  149.4 0.7 reshape.145
  150.1 0.7 fusion.6
  150.8 0.7 reshape.147
  151.5 0.7 reshape.144
  (24 shorter events, 0.2 us)
Async XLA Ops:
  0.6 8.4 %copy-start.11 = (bf16[576,640]{1,0:T(8,128)(2,1)S(1)}, bf16[576,640]{1,0:T(8,128)(2,1)}, u32[]{:S(2)}) copy-start(bf16[576,640]{1,0:T(8,128)(2,1)} %constant.21.clone.stream) | copy-start | bytes 2211844
  0.7 8.9 %copy-start.17 = (bf16[27648]{0:T(1024)(128)(2,1)S(1)}, bf16[27648]{0:T(1024)(128)(2,1)}, u32[]{:S(2)}) copy-start(bf16[27648]{0:T(1024)(128)(2,1)} %param.23) | copy-start | bytes 165892
  0.7 8.8 %copy-start.16 = (bf16[27648]{0:T(1024)(128)(2,1)S(1)}, bf16[27648]{0:T(1024)(128)(2,1)}, u32[]{:S(2)}) copy-start(bf16[27648]{0:T(1024)(128)(2,1)} %param.22) | copy-start | bytes 165892
  4.9 4.9 %copy-start.18 = (bf16[36]{0:T(256)(128)(2,1)S(1)}, bf16[36]{0:T(256)(128)(2,1)}, u32[]{:S(2)}) copy-start(bf16[36]{0:T(256)(128)(2,1)} %param.25) | copy-start | bytes 220
  4.9 5.0 %copy-start.10 = (s32[256]{0:T(256)S(1)}, s32[256]{0:T(256)}, u32[]{:S(2)}) copy-start(s32[256]{0:T(256)} %param.17) | copy-start | bytes 3076
  6.2 3.8 %copy-start.14 = (bf16[256,576]{0,1:T(8,128)(2,1)S(1)}, bf16[256,576]{0,1:T(8,128)(2,1)}, u32[]{:S(2)}) copy-start(bf16[256,576]{0,1:T(8,128)(2,1)} %param.16) | copy-start | bytes 884740
  7.2 3.1 %copy-start.15 = (bf16[256,576]{0,1:T(8,128)(2,1)S(1)}, bf16[256,576]{0,1:T(8,128)(2,1)}, u32[]{:S(2)}) copy-start(bf16[256,576]{0,1:T(8,128)(2,1)} %param.26) | copy-start | bytes 884740
  9.8 61.0 %copy-start.8 = (bf16[2,64,640]{2,1,0:T(8,128)(2,1)S(1)}, bf16[2,64,640]{2,1,0:T(8,128)(2,1)}, u32[]{:S(2)}) copy-start(bf16[2,64,640]{2,1,0:T(8,128)(2,1)} %constant.25.clone.holder) | copy-start | bytes 491524
  9.8 61.0 %copy-start.9 = (bf16[2,64,640]{2,1,0:T(8,128)(2,1)S(1)}, bf16[2,64,640]{2,1,0:T(8,128)(2,1)}, u32[]{:S(2)}) copy-start(bf16[2,64,640]{2,1,0:T(8,128)(2,1)} %constant.24.clone.pick) | copy-start | bytes 491524
  65.7 1.5 copy-start.1
  67.2 1.2 copy-start.5
  68.3 1.2 copy-start.6
  69.5 1.2 copy-start.7
  96.3 1.7 %copy-start = (bf16[32,64,640]{2,1,0:T(8,128)(2,1)S(1)}, bf16[32,64,640]{2,1,0:T(8,128)(2,1)}, u32[]{:S(2)}) copy-start(bf16[32,64,640]{2,1,0:T(8,128)(2,1)} %get-tuple-element.33) | copy-start | bytes 7864324
  98.0 1.4 copy-start.2
  99.4 1.4 copy-start.3
  100.8 1.4 copy-start.4
  102.2 43.5 %copy-start.12 = (bf16[576,640]{1,0:T(8,128)(2,1)S(1)}, bf16[576,640]{1,0:T(8,128)(2,1)}, u32[]{:S(2)}) copy-start(bf16[576,640]{1,0:T(8,128)(2,1)} %constant.21.clone.stream) | copy-start | bytes 2211844
  145.2 4.9 %copy-start.13 = (bf16[576,576]{1,0:T(8,128)(2,1)S(1)}, bf16[576,576]{1,0:T(8,128)(2,1)}, u32[]{:S(2)}) copy-start(bf16[576,576]{1,0:T(8,128)(2,1)} %constant.22.clone) | copy-start | bytes 1990660

commit v4 on v3

--- a/solution.py
+++ b/solution.py
@@ -516,7 +516,7 @@
             pltpu.SemaphoreType.DMA((len(PIECES), 12)),
         ],
         compiler_params=pltpu.CompilerParams(
-            collective_id=0, has_side_effects=True, vmem_limit_bytes=32 * 1024 * 1024
+            collective_id=0, has_side_effects=True, vmem_limit_bytes=12 * 1024 * 1024
         ),
         name="gather_weights",
     )(*parts)
@@ -543,7 +543,7 @@
             pltpu.SemaphoreType.DMA((len(PIECES), 8)),
         ],
         compiler_params=pltpu.CompilerParams(
-            collective_id=1, has_side_effects=True, vmem_limit_bytes=40 * 1024 * 1024
+            collective_id=1, has_side_effects=True, vmem_limit_bytes=20 * 1024 * 1024
         ),
         name="scatter_gradients",
     )(*parts)
@@ -794,7 +794,7 @@
             pltpu.VMEM((count, STREAM), jnp.float32),
             pltpu.VMEM((count, STREAM), jnp.float32),
         ],
-        compiler_params=pltpu.CompilerParams(vmem_limit_bytes=52 * 1024 * 1024),
+        compiler_params=pltpu.CompilerParams(vmem_limit_bytes=34 * 1024 * 1024),
         name="local_layer",
     )(*operands)
 

time: 153 us -> 155 us (1.013)
  local copies, waits for them, and re-layouts: 25.9 us -> 32.8 us
  Pallas kernels: 120 us -> 114 us
    unnamed x42 -> x52, local copies, waits for them, and re-layouts: 13.9 us -> 20.8 us
    pallas_call x1, Pallas kernels: 23.8 us -> 17.7 us  [local_layer(): pl.pallas_call(layer_kernel, out_shape=(jax.ShapeDtypeStruct((count, D),...]
where the time goes in v4:
time: 155 us; the launch traced here: 154 us
  Pallas kernels  114 us (74%)
  local copies, waits for them, and re-layouts  32.8 us (21%)
  matrix products  3.07 us (2%)
  other arithmetic  2.79 us (2%)
    pallas_call x1, Pallas kernels, gather_packed(): pl.pallas_call(gather_kernel, out_shape=tuple((jax.ShapeDtypeStruct(AXIS_...  53.7 us
    pallas_call x1, Pallas kernels, scatter_packed(): pl.pallas_call(scatter_kernel, out_shape=tuple((jax.ShapeDtypeStruct(shap...  43 us
    unnamed x52, local copies, waits for them, and re-layouts  20.8 us
    pallas_call x1, Pallas kernels, local_layer(): pl.pallas_call(layer_kernel, out_shape=(jax.ShapeDtypeStruct((count, D),...  17.7 us

profile of v4, /device:TPU:0, one launch (start us, length us, event | category | flops | bytes accessed | tf_op | source)
XLA Modules:
  0.0 154.0 jit_solution(3175298264728695244)
XLA Ops:
  0.6 0.0 copy-start
  0.7 0.0 copy-start.22
  0.7 0.0 copy-start.21
  0.7 0.9 convert_reduce_fusion
  1.6 0.8 reshape.127
  2.4 0.8 reshape.128
  3.2 0.8 reshape.126
  4.0 0.8 reshape.129
  4.9 0.0 copy-start.23
  4.9 0.0 copy-start.17
  4.9 1.3 fusion.1
  6.2 0.0 copy-start.19
  6.2 0.8 slice.66
  7.1 0.1 slice.67.refs_1_
  7.2 0.0 copy-start.20
  7.2 0.8 slice.68
  8.0 0.1 slice.69.refs_2_
  8.1 0.9 reshape.134
  9.1 0.0 copy-done
  9.1 0.3 fusion
  9.3 0.1 concatenate.29
  9.4 0.0 copy-done.21
  9.5 0.1 reshape.130
  9.6 0.0 copy-done.22
  9.6 0.1 reshape.131
  9.7 0.1 concatenate.30
  9.9 0.1 copy.43.seg_col
  10.0 0.9 copy.41.tokens
  10.9 0.9 copy.42.cotangent
  11.8 0.5 fusion.7
  12.4 0.3 pad_maximum_fusion.2
  12.7 53.7 %gather_weights.1 = (bf16[4,2,2,2,16,1536]{5,4,3,2,1,0:T(8,128)(2,1)S(1)}, bf16[4,2,2,2,16,1536]{5,4,3,2,1,0:T(8,128)(2,1)S(1)}, bf16[4,2,2,2,16,1536]{5,4,3,2,1...) custom-call(bf16[16,1536]{1,0:T(8,128)(2,1)S(1)} %slice.81.refs_0_, bf16[16,1536]{1,0:T(8,128)(2,1)S(1)} %slice.67.refs_1_, ...), custom_call_target="tpu_custom_call" | custom-call | tf_op jit(solution)/shard_map/gather_weights/pallas_call | solution.py:509
  66.3 1.0 copy-done.7
  67.3 1.0 copy-done.8
  68.3 1.0 copy-done.9
  69.3 0.9 copy-done.12
  70.2 0.9 copy-done.13
  71.1 17.7 %local_layer.1 = (bf16[256,576]{1,0:T(8,128)(2,1)S(1)}, bf16[256,576]{1,0:T(8,128)(2,1)S(1)}, bf16[512,1536]{1,0:T(8,128)(2,1)S(1)}, bf16[512,1536]{1,0:T(8,128)...) custom-call(bf16[256,576]{1,0:T(8,128)(2,1)S(1)} %copy-done.7, ...), custom_call_target="tpu_custom_call" | custom-call | tf_op jit(solution)/shard_map/local_layer/pallas_call | solution.py:774
  88.9 1.2 copy-done.1
  90.1 1.1 copy-done.3
  91.2 1.2 copy-done.5
  92.4 0.7 copy-done.10
  93.1 0.7 copy-done.11
  93.9 1.8 %copy.44 = bf16[256,576]{0,1:T(8,128)(2,1)} copy(bf16[256,576]{1,0:T(8,128)(2,1)} %copy-done.11) | data formatting | bytes 589824
  95.7 1.8 %copy.45 = bf16[256,576]{0,1:T(8,128)(2,1)} copy(bf16[256,576]{1,0:T(8,128)(2,1)} %copy-done.10) | data formatting | bytes 589824
  97.6 1.4 copy-done.2
  99.0 1.4 copy-done.4
  100.4 1.4 copy-done.6
  101.8 43.0 %scatter_gradients.1 = (f32[16,1536]{1,0:T(8,128)S(1)}, f32[16,1536]{1,0:T(8,128)S(1)}, f32[16,1536]{1,0:T(8,128)S(1)}, f32[64,640]{1,0:T(8,128)S(1)}) custom-call(bf16[4,2,2,2,16,1536]{5,4,3,2,1,0:T(8,128)(2,1)S(1)} %bitcast.25, bf16[4,2,2,2,16,1536]{5,4,3,2,1,0:T(8,128)(2,1)S(1)} %bitcast.26, bf16[4,2,2,2,16,1536]{5,4,3,2,1,0:T(8,128)(2,1)S(1)} %bitcast.27, ...), custom_call_target="tpu_custom_call" | custom-call | tf_op jit(solution)/shard_map/scatter_gradients/pallas_call | solution.py:535
  144.8 0.0 copy-start.14
  144.8 0.6 copy-done.14
  145.4 0.6 copy-done.16
  146.1 0.5 slice_bitcast_fusion
  146.6 0.7 fusion.3
  147.3 0.7 reshape.150
  148.1 0.9 pad_maximum_fusion.1
  149.0 0.7 reshape.149
  149.7 0.7 reshape.148
  150.4 0.1 fusion.8
  150.4 0.7 reshape.146
  151.1 0.7 reshape.145
  151.8 0.7 fusion.6
  152.5 0.7 reshape.147
  153.3 0.7 reshape.144
  (34 shorter events, 0.2 us)
Async XLA Ops:
  0.6 8.4 %copy-start = (bf16[576,640]{1,0:T(8,128)(2,1)S(1)}, bf16[576,640]{1,0:T(8,128)(2,1)}, u32[]{:S(2)}) copy-start(bf16[576,640]{1,0:T(8,128)(2,1)} %constant.21.clone.stream) | copy-start | bytes 2211844
  0.7 8.9 %copy-start.22 = (bf16[27648]{0:T(1024)(128)(2,1)S(1)}, bf16[27648]{0:T(1024)(128)(2,1)}, u32[]{:S(2)}) copy-start(bf16[27648]{0:T(1024)(128)(2,1)} %param.23) | copy-start | bytes 165892
  0.7 8.8 %copy-start.21 = (bf16[27648]{0:T(1024)(128)(2,1)S(1)}, bf16[27648]{0:T(1024)(128)(2,1)}, u32[]{:S(2)}) copy-start(bf16[27648]{0:T(1024)(128)(2,1)} %param.22) | copy-start | bytes 165892
  4.9 4.9 %copy-start.23 = (bf16[36]{0:T(256)(128)(2,1)S(1)}, bf16[36]{0:T(256)(128)(2,1)}, u32[]{:S(2)}) copy-start(bf16[36]{0:T(256)(128)(2,1)} %param.25) | copy-start | bytes 220
  4.9 5.0 %copy-start.17 = (s32[256]{0:T(256)S(1)}, s32[256]{0:T(256)}, u32[]{:S(2)}) copy-start(s32[256]{0:T(256)} %param.17) | copy-start | bytes 3076
  6.2 3.8 %copy-start.19 = (bf16[256,576]{0,1:T(8,128)(2,1)S(1)}, bf16[256,576]{0,1:T(8,128)(2,1)}, u32[]{:S(2)}) copy-start(bf16[256,576]{0,1:T(8,128)(2,1)} %param.16) | copy-start | bytes 884740
  7.2 3.8 %copy-start.20 = (bf16[256,576]{0,1:T(8,128)(2,1)S(1)}, bf16[256,576]{0,1:T(8,128)(2,1)}, u32[]{:S(2)}) copy-start(bf16[256,576]{0,1:T(8,128)(2,1)} %param.26) | copy-start | bytes 884740
  66.3 1.0 copy-start.7
  67.3 1.0 copy-start.8
  68.3 1.0 copy-start.9
  69.3 0.9 copy-start.12
  70.2 0.9 copy-start.13
  88.9 1.2 copy-start.1
  90.1 1.1 copy-start.3
  91.2 1.2 copy-start.5
  92.4 0.7 copy-start.10
  93.1 0.7 copy-start.11
  97.6 1.4 copy-start.2
  99.0 1.4 copy-start.4
  100.4 1.4 copy-start.6
  144.8 0.6 copy-start.14
  145.4 0.6 copy-start.16
  146.1 5.7 %copy-start.18 = (bf16[576,576]{1,0:T(8,128)(2,1)S(1)}, bf16[576,576]{1,0:T(8,128)(2,1)}, u32[]{:S(2)}) copy-start(bf16[576,576]{1,0:T(8,128)(2,1)} %constant.22.clone) | copy-start | bytes 1990660
  146.1 3.6 %copy-start.15 = (f32[16,1536]{1,0:T(8,128)S(1)}, f32[16,1536]{1,0:T(8,128)}, u32[]{:S(2)}) copy-start(f32[16,1536]{1,0:T(8,128)} %copy-done.14) | copy-start | bytes 294916
